TPU v7x, 256 devices: a whole 4x4x8 slice. The times are simulated.
256 devices in a mesh: mem: 8 (over y, core), tile: 32 (over x, z).
Axes of the slice: x: 4, y: 4, z: 8, core: 2. Of those that a mesh axis runs over, the one named last changes fastest.
Arguments:
- atmos: float32 [64, 2048, 1024], P('mem', 'tile'), parts along dimension 0, may hold values from -6 to 6
- kappa: float32 [2048, 1024], P('tile'), may hold values from 0.02 to 0.24
- weights: bfloat16 [16384, 128, 128], P('tile'), may hold values from -0.5 to 0.5
- pair_land: int32 [16384], P('tile'), may hold values from 0 to 4095, as said below
- pair_atm: int32 [16384], P('tile'), may hold values from 0 to 511
- land_mask: int32 [4096], P('tile'), may hold values 0 or 1
Outputs:
- land: float32 [4096, 64, 128], P('tile', 'mem'), parts along dimension 1
There are 8 independent parts, one for each index of `mem`. A program takes and returns all parts, laid end to end along the dimension named above; an argument that names none is the same for every part. Nothing has to cross between parts.
Inputs may be any that keep to these rules, and one draw needn't show every extreme that they name: `pair_land`: of the 512 pairs of one device, at most 32 write land blocks of any one device's range d * 128 to (d+1) * 128 - 1; one range, drawn from the seed, receives exactly 32 from every device.
All inputs are finite; a program needn't handle non-finite values. No bound on the sum of `land_mask` on one device may be relied on, other than what follows from the above.
Results may differ from a plain program's by a relative error of at most 0.0029.
Values sent between devices are 32-bit elements; how exact they have to be, the bound alone decides.
No kernel may reach another device: no remote copies, remote signals or barrier semaphores. Data moves between devices by JAX's collectives and lax.ppermute only.
A program may use at most 128 MiB of HBM per device.

v0:
```python
import jax
import jax.numpy as jnp
from jax import lax
from jax.sharding import PartitionSpec as P


def padded(cells, sides, width):
    for axis, dim in sides:
        count = lax.axis_size(axis)
        ends = count - 1
        head = lax.slice_in_dim(cells, 0, width, axis=dim)
        tail = lax.slice_in_dim(cells, cells.shape[dim] - width, cells.shape[dim], axis=dim)
        cells = jnp.concatenate(
            [
                lax.ppermute(tail, axis, [(i, (i + 1) % count) for i in range(ends)]),
                cells,
                lax.ppermute(head, axis, [((i + 1) % count, i) for i in range(ends)]),
            ],
            axis=dim,
        )
    return cells


def laplace_step(center, north, south, coeff):
    east = jnp.roll(center, -1, axis=2)
    west = jnp.roll(center, 1, axis=2)
    return center + coeff[None] * (north + south + east + west - 4.0 * center)


def gather_border_cells(atmos):
    return padded(atmos, (("tile", 1),), 1)


def body(atmos, kappa, weights, pair_land, pair_atm, land_mask):
    member_field_stack = atmos.shape[0]
    block = weights.shape[1]
    pair_count = weights.shape[0]
    land_tile_count = land_mask.shape[0]
    extended = gather_border_cells(atmos)
    smoothed = laplace_step(atmos, extended[:, :-2, :], extended[:, 2:, :], kappa)
    smoothed = smoothed.astype(jnp.bfloat16)
    blocks = smoothed.reshape(member_field_stack, -1, block).transpose(1, 0, 2)
    selected_pairs = jnp.take(blocks, pair_atm, axis=0)
    remap_contribution_part = jnp.einsum(
        "tuv,tvi->tui", selected_pairs, weights, preferred_element_type=jnp.float32
    )
    remap_contribution_part = remap_contribution_part.reshape(
        pair_count, member_field_stack * block
    )
    targets = jnp.arange(lax.axis_size("tile") * land_tile_count, dtype=jnp.int32)
    select = (pair_land[None, :] == targets[:, None]).astype(jnp.float32)
    summed = lax.psum_scatter(
        jnp.dot(select, remap_contribution_part, precision=lax.Precision.HIGHEST),
        "tile",
        scatter_dimension=0,
        tiled=True,
    )
    kept = summed * land_mask.astype(jnp.float32)[:, None]
    return kept.reshape(land_tile_count, member_field_stack, block)


def solution(mesh):
    in_specs = (
        P("mem", "tile", None),
        P("tile", None),
        P("tile", None, None),
        P("tile"),
        P("tile"),
        P("tile"),
    )
    out_specs = P("tile", "mem", None)
    return jax.shard_map(body, mesh=mesh, in_specs=in_specs, out_specs=out_specs, check_vma=False)
```

profile of v0, /device:TPU:6, one launch (start us, length us, event | category | flops | bytes accessed | tf_op | source)
XLA Modules:
  0.0 303.3 jit_solution(10698541996191909858)
XLA Ops:
  6.5 0.0 reduce-scatter.2.cloned.1.call-start
  6.5 1.1 fusion.18
  7.6 3.8 %collective-permute-start = (f32[8,1,1024]{2,1,0:T(1,128)S(1)}, f32[8,1,1024]{2,1,0:T(1,128)S(1)}, u32[]{:S(2)}, u32[]{:S(2)}) collective-permute-start(f32[8,1,1024]{2,1,0:T(1,128)S(1)} %get-tuple-element.9), channel_id=1, source_target_pairs={{0,1},{1,2},{2,3},{3,4},{4,5},{5,6},{6,7},{7,8},{8,9},{9,10},{10,1... | collective-permute-start | bytes 98312 | tf_op jit(solution)/shard_map/ppermute | solution.py:15
  11.5 0.0 copy-start
  11.5 0.0 copy-start.2
  11.5 0.0 copy-start.1
  11.5 6.3 %collective-permute-start.1 = (f32[8,1,1024]{2,1,0:T(1,128)S(1)}, f32[8,1,1024]{2,1,0:T(1,128)S(1)}, u32[]{:S(2)}, u32[]{:S(2)}) collective-permute-start(f32[8,1,1024]{2,1,0:T(1,128)S(1)} %get-tuple-element.10), channel_id=1, source_target_pairs={{1,0},{2,1},{3,2},{4,3},{5,4},{6,5},{7,6},{8,7},{9,8},{10,9},{11,1... | collective-permute-start | bytes 98312 | tf_op jit(solution)/shard_map/ppermute | solution.py:17
  17.8 3.0 fusion.17
  20.7 0.0 copy-done
  20.7 0.1 fusion.16
  20.9 0.0 copy-done.2
  20.9 0.0 collective-permute-done
  21.0 0.0 collective-permute-done.1
  21.0 0.0 copy-done.1
  21.0 1.2 fusion.10
  22.2 0.5 reshape.17
  22.7 0.7 copy.15
  23.3 1.8 gather_fusion
  25.1 0.0 copy-start.3
  25.2 8.4 %fusion.11 = f32[512,8,128]{2,1,0:T(8,128)S(1)} fusion(bf16[512,128,128]{2,1,0:T(8,128)(2,1)} %param.8, bf16[512,8,128]{2,1,0:T(8,128)(2,1)S(1)} %gather_fusion, pred[512]{0:T(512)(128)(4,1)S(1)} %compare_and_fusion), kind=kOutput, calls=%fused_computation.16 | convolution fusion | flops 134742016 | bytes 19923456 | tf_op jit(solution)/shard_map/tuv,tvi->tui/dot_general | solution.py:44
  33.6 0.0 copy-done.3
  33.6 16.5 %fusion = f32[4096,1024]{1,0:T(8,128)} fusion(s32[512]{0:T(512)S(1)} %copy-done.3, f32[64,8,8,128]{3,2,1,0:T(8,128)S(1)} %bitcast.11), kind=kOutput, calls=%fused_computation.2 | convolution fusion | flops 25771900928 | bytes 18876416 | tf_op jit(solution)/shard_map/dot_general | solution.py:53
  50.1 0.0 copy-start.4
  50.1 0.0 reduce-scatter.2.cloned.1.call-update
  50.1 0.6 copy-done.4
  50.8 243.6 %reduce-scatter.2.cloned.1.call-done = f32[128,1024]{1,0:T(8,128)} async-done(((f32[4096,1024]{1,0:T(8,128)}), f32[128,1024]{1,0:T(8,128)}) %reduce-scatter.2.cloned.1.call-update) | async-done | bytes 524304 | tf_op jit(solution)/shard_map/reduce_scatter | solution.py:52
  294.4 1.1 multiply_bitcast_fusion
  295.5 0.9 copy.9
  (4 shorter events, 0.0 us)
Async XLA Ops:
  6.5 287.8 %reduce-scatter.2.cloned.1.call-start = ((), (), s32[]{:S(2)}) async-start(), calls=%async_computation.1 | async-start | bytes 17301504 | tf_op jit(solution)/shard_map/reduce_scatter | solution.py:52
  7.6 13.3 %collective-permute-start = (f32[8,1,1024]{2,1,0:T(1,128)S(1)}, f32[8,1,1024]{2,1,0:T(1,128)S(1)}, u32[]{:S(2)}, u32[]{:S(2)}) collective-permute-start(f32[8,1,1024]{2,1,0:T(1,128)S(1)} %get-tuple-element.9), channel_id=1, source_target_pairs={{0,1},{1,2},{2,3},{3,4},{4,5},{5,6},{6,7},{7,8},{8,9},{9,10},{10,1... | collective-permute-start | bytes 98312 | tf_op jit(solution)/shard_map/ppermute | solution.py:15
  11.5 9.3 %copy-start = (f32[8,64,1024]{2,1,0:T(8,128)S(1)}, f32[8,64,1024]{2,1,0:T(8,128)}, u32[]{:S(2)}) copy-start(f32[8,64,1024]{2,1,0:T(8,128)} %param.6) | copy-start | bytes 6291460
  11.5 9.4 %copy-start.2 = (s32[512]{0:T(512)S(1)}, s32[512]{0:T(512)}, u32[]{:S(2)}) copy-start(s32[512]{0:T(512)} %param.10) | copy-start | bytes 6148
  11.5 9.5 %copy-start.1 = (f32[64,1024]{1,0:T(8,128)S(1)}, f32[64,1024]{1,0:T(8,128)}, u32[]{:S(2)}) copy-start(f32[64,1024]{1,0:T(8,128)} %param.7) | copy-start | bytes 786436
  11.5 9.5 %collective-permute-start.1 = (f32[8,1,1024]{2,1,0:T(1,128)S(1)}, f32[8,1,1024]{2,1,0:T(1,128)S(1)}, u32[]{:S(2)}, u32[]{:S(2)}) collective-permute-start(f32[8,1,1024]{2,1,0:T(1,128)S(1)} %get-tuple-element.10), channel_id=1, source_target_pairs={{1,0},{2,1},{3,2},{4,3},{5,4},{6,5},{7,6},{8,7},{9,8},{10,9},{11,1... | collective-permute-start | bytes 98312 | tf_op jit(solution)/shard_map/ppermute | solution.py:17
  25.1 8.4 %copy-start.3 = (s32[512]{0:T(512)S(1)}, s32[512]{0:T(512)}, u32[]{:S(2)}) copy-start(s32[512]{0:T(512)} %param.9) | copy-start | bytes 6148
  50.1 0.7 copy-start.4
Sparse Core Ops, SparseCore 0:
  50.2 244.0 reduce-scatter.1
where the time goes:
time: 304 us; the launch traced here: 303 us
  waiting for transfers between devices  244 us (80%)
  matrix products  24.9 us (8%)
  between operations  13.6 us (4%)
  starting transfers between devices  10.1 us (3%)
  local copies, waits for them, and re-layouts  8.71 us (3%)
    reduce_scatter x1, waiting for transfers between devices, body(): lax.psum_scatter(jnp.dot(select, remap_contribution_part, precision=lax.P...  244 us
    dot_general x1, matrix products, body(): jnp.dot(select, remap_contribution_part, precision=lax.Precision.HIGHEST)  16.5 us
    dot_general x1, matrix products, body(): jnp.einsum('tuv,tvi->tui', selected_pairs, weights, preferred_element_typ...  8.43 us
    ppermute x1, starting transfers between devices, padded(): lax.ppermute(head, axis, [((i + 1) % count, i) for i in range(ends)])  6.26 us
  transfers between devices with their start and end apart: 3, of which 1 were waited for; matrix products, arithmetic and copies ran while one was open for 1% of the time, Pallas kernels for 0%

commit v1 on v0

v1 whole, which is shorter than its diff:
```python
import jax
import jax.numpy as jnp
from jax import lax
from jax.experimental import pallas as pl
from jax.experimental.pallas import tpu as pltpu
from jax.sharding import PartitionSpec as P

X, Z = 4, 8
F, B = 8, 128
ROWS, COLS = 64, 1024
LAND = 128
PAIRS = 512
CAP = 32
EMPTY = 2 * LAND
GROUP = 16
PART = 32
WEIGHT_PARTS = PAIRS // PART
FAR_VMEM, NEAR_VMEM = 56, 48
DISTANCES = (4, 3, 2, 1, 0)
SIZES = (CAP, 2 * CAP, 2 * CAP, 2 * CAP, CAP)
STARTS = tuple(X * (sum(SIZES[:n]) + n) for n in range(len(SIZES) + 1))
BITS = 9
LAND_BITS = 12


def shift(dx, dz):
    return [
        (x * Z + z, ((x + dx) % X) * Z + (z + dz) % Z) for x in range(X) for z in range(Z)
    ]


def send_x(a, dx):
    return lax.ppermute(a, "tile", shift(dx, 0))


def send_z(a, dz):
    return lax.ppermute(a, "tile", shift(0, dz))


def make_plan(packed, jobs_ref, order_ref, bounds_ref, table_ref):
    land, atm = packed & ((1 << LAND_BITS) - 1), packed >> LAND_BITS
    t = lax.axis_index("tile")
    x, z = t // Z, t % Z
    owner, row = land >> 7, land & (LAND - 1)
    ex = ((owner >> 3) - x) & (X - 1)
    delta = ((owner & (Z - 1)) - z) & (Z - 1)
    dist = jnp.minimum(delta, Z - delta)
    start = jnp.zeros_like(dist)
    for n, d in enumerate(DISTANCES):
        start = jnp.where(dist == d, STARTS[n] + ex * (SIZES[n] + 1), start)
    bounds_ref[0] = jnp.sum((start < STARTS[1]).astype(jnp.int32))
    target = row + jnp.where(delta > 4, LAND, 0) - EMPTY

    def column(a):
        return jnp.transpose(jnp.broadcast_to(a, (F, PAIRS)))[:, 0:1]

    def total(a):
        return jnp.sum(a, axis=0, keepdims=True)

    square = (PAIRS, PAIRS)
    p_row = lax.broadcasted_iota(jnp.int32, (1, PAIRS), 1)
    earlier = lax.broadcasted_iota(jnp.int32, square, 0) < lax.broadcasted_iota(
        jnp.int32, square, 1
    )
    start_col = column(start)
    one = jnp.ones(square, jnp.int32)
    nil = jnp.zeros(square, jnp.int32)
    rank = total(jnp.where((start_col == start) & earlier, one, nil))
    place = rank + total(jnp.where(start_col < start, one, nil))
    slot = start + rank
    job = p_row + (atm << BITS) + (slot << (2 * BITS))
    jobs_ref[...] = job
    order_ref[...] = total(jnp.where(column(place) == p_row, column(job), 0))
    slot_col, target_col = column(slot), column(target)
    lane = lax.broadcasted_iota(jnp.int32, (1, B), 1)
    for n in range(len(SIZES)):
        for m in range(X // 2):
            head = STARTS[n] + 2 * m * (SIZES[n] + 1)
            spot = jnp.where(lane < B // 2, head + lane, head + SIZES[n] + 1 + lane - B // 2)
            spot = jnp.where(lane % (B // 2) < SIZES[n], spot, -1)
            hit = total(jnp.where(slot_col == spot, target_col, 0))
            k = n * (X // 2) + m
            table_ref[k : k + 1] = (EMPTY + hit).astype(jnp.float32)


def start_weights(w_ref, w, sem):
    for n in range(WEIGHT_PARTS):
        at = pl.ds(n * PART, PART)
        pltpu.make_async_copy(w_ref.at[at], w.at[at], sem.at[n]).start()


def wait_weights(w_ref, w, sem, n):
    at = pl.ds(n * PART, PART)
    pltpu.make_async_copy(w_ref.at[at], w.at[at], sem.at[n]).wait()


def put_targets(table, send, first, last, base):
    for n in range(first, last):
        for e in range(X):
            end = STARTS[n] + (e + 1) * (SIZES[n] + 1) - 1 - base
            k = n * (X // 2) + e // 2
            send[end, 0:1] = table[k : k + 1]


def put_messages(send, outs, sem, first, last, base):
    copies = []
    for n in range(first, last):
        for e in range(X):
            at = STARTS[n] + e * (SIZES[n] + 1) - base
            k = len(copies)
            copies.append(
                pltpu.make_async_copy(send.at[pl.ds(at, SIZES[n] + 1)], outs[k], sem.at[k])
            )
    for c in copies:
        c.start()
    for c in copies:
        c.wait()


def far_kernel(
    atmos, kappa, packed, north, south, w_ref, smooth, jobs, table, *rest
):
    *outs, field, coeff, pairs, edge, rows, order, place, bounds, w, send, w_sem, out_sem, sem = rest
    per = COLS // B
    small = pltpu.make_async_copy(packed, pairs, sem.at[per])
    small.start()
    copies = [
        pltpu.make_async_copy(atmos.at[:, pl.ds(c * B, B)], field.at[c], sem.at[c])
        for c in range(per)
    ] + [
        pltpu.make_async_copy(kappa, coeff, sem.at[per + 1]),
        pltpu.make_async_copy(north, edge.at[0], sem.at[per + 2]),
        pltpu.make_async_copy(south, edge.at[1], sem.at[per + 3]),
    ]
    for c in copies:
        c.start()
    start_weights(w_ref, w, w_sem)
    small.wait()
    make_plan(pairs[...], jobs, order, bounds, table)
    to_smem = pltpu.make_async_copy(order, place, sem.at[per])
    to_smem.start()
    for c in copies:
        c.wait()
    tile = lax.axis_index("tile")
    above = jnp.where(tile > 0, edge[0], 0.0)
    under = jnp.where(tile < X * Z - 1, edge[1], 0.0)

    def row(r):
        return jnp.concatenate([field[c, pl.ds(r, F, stride=ROWS), :] for c in range(per)], axis=1)

    def step(r, carry):
        prev, cur = carry
        nxt = row(jnp.minimum(r + 1, ROWS - 1))
        below = jnp.where(r < ROWS - 1, nxt, under)
        east = pltpu.roll(cur, COLS - 1, 1)
        west = pltpu.roll(cur, 1, 1)
        value = cur + coeff[pl.ds(r, 1), :] * (prev + below + east + west - 4.0 * cur)
        for c in range(per):
            rows[r * per + c] = value[:, c * B : (c + 1) * B]
        return cur, nxt

    lax.fori_loop(0, ROWS, step, (above, row(0)), unroll=2)
    save = pltpu.make_async_copy(rows, smooth, sem.at[0])
    save.start()
    put_targets(table, send, 0, 1, 0)
    to_smem.wait()
    for n in range(WEIGHT_PARTS):
        wait_weights(w_ref, w, w_sem, n)
    mask = (1 << BITS) - 1
    high = bounds[0]

    def multiply(n, carry):
        for j in range(GROUP):
            job = place[0, jnp.minimum(n * GROUP + j, high - 1)]
            block = rows[(job >> BITS) & mask].astype(jnp.bfloat16)
            send[job >> (2 * BITS)] = jnp.dot(
                block, w[job & mask], preferred_element_type=jnp.float32
            )
        return carry

    lax.fori_loop(0, (high + GROUP - 1) // GROUP, multiply, 0)
    put_messages(send, outs, out_sem, 0, 1, 0)
    save.wait()


def near_kernel(jobs, table, smooth, w_ref, *rest):
    *outs, rows, w, send, w_sem, out_sem, sem = rest
    base = STARTS[1] - 1
    start_weights(w_ref, w, w_sem)
    load = pltpu.make_async_copy(smooth, rows, sem)
    load.start()
    put_targets(table, send, 1, len(SIZES), base)
    load.wait()
    mask = (1 << BITS) - 1

    def multiply(n, carry):
        wait_weights(w_ref, w, w_sem, n)
        for j in range(PART):
            p = n * PART + j
            job = jobs[0, p]
            block = rows[(job >> BITS) & mask].astype(jnp.bfloat16)
            send[jnp.maximum((job >> (2 * BITS)) - base, 0)] = jnp.dot(
                block, w[p], preferred_element_type=jnp.float32
            )
        return carry

    lax.fori_loop(0, WEIGHT_PARTS, multiply, 0)
    put_messages(send, outs, out_sem, 1, len(SIZES), base)


def messages(first, last):
    return [
        jax.ShapeDtypeStruct((SIZES[n] + 1, F, B), jnp.float32)
        for n in range(first, last)
        for _ in range(X)
    ]


def remap_far(atmos, kappa, packed, north, south, weights):
    vmem, anywhere = (pl.BlockSpec(memory_space=m) for m in (pltpu.VMEM, pl.ANY))
    shapes = messages(0, 1)
    smooth, jobs, table, *outs = pl.pallas_call(
        far_kernel,
        out_shape=[
            jax.ShapeDtypeStruct((ROWS * COLS // B, F, B), jnp.float32),
            jax.ShapeDtypeStruct((1, PAIRS), jnp.int32),
            jax.ShapeDtypeStruct((len(SIZES) * X // 2, B), jnp.float32),
        ]
        + shapes,
        in_specs=[anywhere] * 6,
        out_specs=[anywhere, vmem, vmem] + [anywhere] * len(shapes),
        scratch_shapes=[
            pltpu.VMEM((COLS // B, F * ROWS, B), jnp.float32),
            pltpu.VMEM((ROWS, COLS), jnp.float32),
            pltpu.VMEM((1, PAIRS), jnp.int32),
            pltpu.VMEM((2, F, COLS), jnp.float32),
            pltpu.VMEM((ROWS * COLS // B, F, B), jnp.float32),
            pltpu.VMEM((1, PAIRS), jnp.int32),
            pltpu.SMEM((1, PAIRS), jnp.int32),
            pltpu.SMEM((1,), jnp.int32),
            pltpu.VMEM((PAIRS, B, B), jnp.bfloat16),
            pltpu.VMEM((STARTS[1], F, B), jnp.float32),
            pltpu.SemaphoreType.DMA((WEIGHT_PARTS,)),
            pltpu.SemaphoreType.DMA((len(shapes),)),
            pltpu.SemaphoreType.DMA((COLS // B + 4,)),
        ],
        compiler_params=pltpu.CompilerParams(vmem_limit_bytes=FAR_VMEM << 20),
        cost_estimate=pl.CostEstimate(flops=1 << 20, bytes_accessed=20 << 20, transcendentals=0),
    )(atmos.reshape(F * ROWS, COLS), kappa, packed, north, south, weights)
    return smooth, jobs, table, outs


def remap_near(jobs, table, smooth, weights):
    smem, vmem, anywhere = (
        pl.BlockSpec(memory_space=m) for m in (pltpu.SMEM, pltpu.VMEM, pl.ANY)
    )
    shapes = messages(1, len(SIZES))
    return pl.pallas_call(
        near_kernel,
        out_shape=shapes,
        in_specs=[smem, vmem, anywhere, anywhere],
        out_specs=[anywhere] * len(shapes),
        scratch_shapes=[
            pltpu.VMEM((ROWS * COLS // B, F, B), jnp.float32),
            pltpu.VMEM((PAIRS, B, B), jnp.bfloat16),
            pltpu.VMEM((STARTS[-1] - STARTS[1] + 1, F, B), jnp.float32),
            pltpu.SemaphoreType.DMA((WEIGHT_PARTS,)),
            pltpu.SemaphoreType.DMA((len(shapes),)),
            pltpu.SemaphoreType.DMA,
        ],
        compiler_params=pltpu.CompilerParams(vmem_limit_bytes=NEAR_VMEM << 20),
        cost_estimate=pl.CostEstimate(flops=1 << 20, bytes_accessed=24 << 20, transcendentals=0),
    )(jobs, table, smooth, weights)


def gather_kernel(size, a0, a1, a2, a3, out, wide, index, sem):
    for n, a in enumerate((a0, a1, a2, a3)):
        wide[n : n + 1] = a[size, 0:1].astype(jnp.int32)
    copy = pltpu.make_async_copy(wide, index, sem)
    copy.start()
    out[...] = jnp.zeros_like(out)
    copy.wait()
    for n, a in enumerate((a0, a1, a2, a3)):

        def add(s, carry, n=n, a=a):
            out[index[n, s + (n % 2) * (B // 2)]] += a[s]
            return carry

        lax.fori_loop(0, size, add, 0, unroll=8)


def gather_class(size, slots):
    return pl.pallas_call(
        lambda *refs: gather_kernel(size, *refs),
        out_shape=jax.ShapeDtypeStruct((EMPTY + 8, F, B), jnp.float32),
        in_specs=[pl.BlockSpec(memory_space=pltpu.VMEM)] * X,
        out_specs=pl.BlockSpec(memory_space=pltpu.VMEM),
        scratch_shapes=[
            pltpu.VMEM((F, B), jnp.int32),
            pltpu.SMEM((F, B), jnp.int32),
            pltpu.SemaphoreType.DMA,
        ],
        compiler_params=pltpu.CompilerParams(vmem_limit_bytes=2 << 20),
        cost_estimate=pl.CostEstimate(
            flops=1 << 32, bytes_accessed=1 << 20, transcendentals=0
        ),
    )(*slots)


def body(atmos, kappa, weights, pair_land, pair_atm, land_mask):
    tiles = X * Z
    north = lax.ppermute(atmos[:, -1, :], "tile", [(i, (i + 1) % tiles) for i in range(tiles)])
    south = lax.ppermute(atmos[:, 0, :], "tile", [((i + 1) % tiles, i) for i in range(tiles)])
    packed = (pair_land + (pair_atm << LAND_BITS)).reshape(1, PAIRS)
    smooth, jobs, table, out = remap_far(atmos, kappa, packed, north, south, weights)
    near = remap_near(jobs, table, smooth, weights)
    sends = [out] + [near[n * X : (n + 1) * X] for n in range(len(SIZES) - 1)]
    dense = {}
    came = None
    for n, (own, *away) in enumerate(sends):
        if came is not None:
            came, away = zip(*(lax.optimization_barrier(both) for both in zip(came, away)))
            dense[DISTANCES[n - 1]] = gather_class(SIZES[n - 1], [mine, *came])
        came, mine = [send_x(a, ex + 1) for ex, a in enumerate(away)], own
    dense[0] = gather_class(SIZES[-1], [mine, *came])
    half = LAND // 2
    pad = ((0, half), (0, 0), (0, 0))
    plus, minus = send_z(dense[4][:half], 1), send_z(dense[4][half:LAND], -1)
    plus, minus = jnp.pad(plus, pad), jnp.pad(minus, (pad[0][::-1], pad[1], pad[2]))
    for k in (3, 2, 1):
        plus = send_z(dense[k][:LAND] + plus, 1)
        minus = send_z(dense[k][LAND : 2 * LAND] + minus, -1)
    total = dense[0][:LAND] + plus + minus
    return total * land_mask.astype(jnp.float32)[:, None, None]


def solution(mesh):
    in_specs = (
        P("mem", "tile", None),
        P("tile", None),
        P("tile", None, None),
        P("tile"),
        P("tile"),
        P("tile"),
    )
    out_specs = P("tile", "mem", None)
    return jax.shard_map(body, mesh=mesh, in_specs=in_specs, out_specs=out_specs, check_vma=False)
```

time: 304 us -> 103 us (0.34)
  the two profiles are of different devices: /device:TPU:6 before, /device:TPU:2 now
where the time goes in v1:
time: 103 us
  starting transfers between devices  41.9 us (41%)
  Pallas kernels  31.4 us (30%)
  waiting for transfers between devices  22.1 us (21%)
  local copies, waits for them, and re-layouts  4.67 us (5%)
  other arithmetic  2.71 us (3%)
    ppermute x15, starting transfers between devices, send_x(): return lax.ppermute(a, 'tile', shift(dx, 0))  20.1 us
    ppermute x8, starting transfers between devices, send_z(): return lax.ppermute(a, 'tile', shift(0, dz))  15.8 us
    ppermute x8, waiting for transfers between devices, send_z(): return lax.ppermute(a, 'tile', shift(0, dz))  15.7 us
    pallas_call x1, Pallas kernels, remap_far(): pl.pallas_call(far_kernel, out_shape=[jax.ShapeDtypeStruct((ROWS * COLS /...  13.2 us
    pallas_call x1, Pallas kernels, remap_near(): pl.pallas_call(near_kernel, out_shape=shapes, in_specs=[smem, vmem, anywh...  9.49 us
    pallas_call x5, Pallas kernels, gather_class(): pl.pallas_call(lambda *refs: gather_kernel(size, *refs), out_shape=jax.Sh...  8.73 us
    ppermute x15, waiting for transfers between devices, send_x(): return lax.ppermute(a, 'tile', shift(dx, 0))  5.9 us
    ppermute x1, starting transfers between devices, body(): lax.ppermute(atmos[:, 0, :], 'tile', [((i + 1) % tiles, i) for i in range...  4.01 us
  transfers between devices with their start and end apart: 25, of which 6 were waited for; matrix products, arithmetic and copies ran while one was open for 2% of the time, Pallas kernels for 18%

profile of v1, /device:TPU:2, one launch (start us, length us, event | category | flops | bytes accessed | tf_op | source)
XLA Modules:
  0.0 103.0 jit_solution(9001242341071897917)
XLA Ops:
  0.0 1.1 %fusion.2 = (f32[8,1,1024]{2,1,0:T(1,128)S(1)}, f32[8,1,1024]{2,1,0:T(1,128)S(1)}) fusion(f32[8,64,1024]{2,1,0:T(8,128)} %param.6), kind=kLoop, calls=%fused_computation.12 | loop fusion | bytes 131072 | tf_op jit(solution)/shard_map/slice | solution.py:313
  1.1 2.0 %collective-permute-start = (f32[8,1024]{1,0:T(8,128)S(1)}, f32[8,1024]{1,0:T(8,128)S(1)}, u32[]{:S(2)}, u32[]{:S(2)}) collective-permute-start(f32[8,1024]{1,0:T(8,128)S(1)} %bitcast.9), channel_id=1, source_target_pairs={{0,1},{1,2},{2,3},{3,4},{4,5},{5,6},{6,7},{7,8},{8,9},{9,10},{10,1... | collective-permute-start | bytes 98312 | tf_op jit(solution)/shard_map/ppermute | solution.py:312
  3.1 4.0 %collective-permute-start.1 = (f32[8,1024]{1,0:T(8,128)S(1)}, f32[8,1024]{1,0:T(8,128)S(1)}, u32[]{:S(2)}, u32[]{:S(2)}) collective-permute-start(f32[8,1024]{1,0:T(8,128)S(1)} %bitcast.10), channel_id=1, source_target_pairs={{1,0},{2,1},{3,2},{4,3},{5,4},{6,5},{7,6},{8,7},{9,8},{10,9},{11,1... | collective-permute-start | bytes 98312 | tf_op jit(solution)/shard_map/ppermute | solution.py:313
  7.1 1.3 %shift-left_add_fusion = s32[512]{0:T(512)} fusion(s32[512]{0:T(512)} %param.9, s32[512]{0:T(512)} %param.10), kind=kLoop, calls=%fused_computation.11 | loop fusion | flops 1024 | bytes 6144 | tf_op jit(solution)/shard_map/add | solution.py:314
  9.5 13.2 %shard_map.64 = (f32[512,8,128]{2,1,0:T(8,128)}, s32[1,512]{1,0:T(1,128)}, f32[10,128]{1,0:T(8,128)}, f32[33,8,128]{2,1,0:T(8,128)}, f32[33,8,128]{2,1,0:T(8,128...) custom-call(f32[512,1024]{1,0:T(8,128)} %bitcast.8, f32[64,1024]{1,0:T(8,128)} %kappa.1, s32[1,512]{1,0:T(1,128)} %bitcast.11, ...), custom_call_target="tpu_custom_call" | custom-call | flops 1048576 | bytes 20971520 | tf_op jit(solution)/shard_map/pallas_call | solution.py:222
  22.7 2.6 %collective-permute-start.12 = (f32[33,8,128]{2,1,0:T(8,128)}, f32[33,8,128]{2,1,0:T(8,128)S(1)}, u32[]{:S(2)}, u32[]{:S(2)}) collective-permute-start(f32[33,8,128]{2,1,0:T(8,128)} %get-tuple-element.74), channel_id=1, source_target_pairs={{0,24},{1,25},{2,26},{3,27},{4,28},{5,29},{6,30},{7,31},{8,0},{9,1... | collective-permute-start | bytes 405512 | tf_op jit(solution)/shard_map/ppermute | solution.py:33
  25.5 2.1 %collective-permute-start.2 = (f32[33,8,128]{2,1,0:T(8,128)}, f32[33,8,128]{2,1,0:T(8,128)S(1)}, u32[]{:S(2)}, u32[]{:S(2)}) collective-permute-start(f32[33,8,128]{2,1,0:T(8,128)} %get-tuple-element.56), channel_id=1, source_target_pairs={{0,8},{1,9},{2,10},{3,11},{4,12},{5,13},{6,14},{7,15},{8,16},{9,17... | collective-permute-start | bytes 405512 | tf_op jit(solution)/shard_map/ppermute | solution.py:33
  27.6 1.6 %copy-done = f32[512,8,128]{2,1,0:T(8,128)S(1)} copy-done((f32[512,8,128]{2,1,0:T(8,128)S(1)}, f32[512,8,128]{2,1,0:T(8,128)}, u32[]{:S(2)}) %copy-start) | copy-done | bytes 2097176
  30.5 9.5 %shard_map.65 = (f32[65,8,128]{2,1,0:T(8,128)S(1)}, f32[65,8,128]{2,1,0:T(8,128)S(1)}, f32[65,8,128]{2,1,0:T(8,128)S(1)}, f32[65,8,128]{2,1,0:T(8,128)S(1)}, f32...) custom-call(s32[1,512]{1,0:T(1,128)S(1)} %copy-done.2, ...), custom_call_target="tpu_custom_call" | custom-call | flops 1048576 | bytes 25165824 | tf_op jit(solution)/shard_map/pallas_call | solution.py:258
  40.1 3.2 %collective-permute-start.8 = (f32[65,8,128]{2,1,0:T(8,128)S(1)}, f32[65,8,128]{2,1,0:T(8,128)S(1)}, u32[]{:S(2)}, u32[]{:S(2)}) collective-permute-start(f32[65,8,128]{2,1,0:T(8,128)S(1)} %get-tuple-element.67), channel_id=1, source_target_pairs={{0,16},{1,17},{2,18},{3,19},{4,20},{5,21},{6,22},{7,23},{8,24},{9,... | collective-permute-start | bytes 798728 | tf_op jit(solution)/shard_map/ppermute | solution.py:33
  43.4 0.7 collective-permute-start.3
  44.1 1.3 %shard_map.70 = f32[264,8,128]{2,1,0:T(8,128)S(1)} custom-call(f32[33,8,128]{2,1,0:T(8,128)S(1)} %copy-done.3, f32[33,8,128]{2,1,0:T(8,128)S(1)} %collective-permute-done.2.refs_1_, f32[33,8,128]{2,1,0:T(8,128)S(1)} %collective-permute-done.7.refs_2_, f32[33,8,128]{2,1,0:T(8,128)S(1)} %collective-permute-done.12.refs_3_), custom_call_target="tpu_custom_call" | custom-call | flops 4294967296 | bytes 1048576 | tf_op jit(solution)/shard_map/pallas_call | solution.py:293
  45.7 4.4 %collective-permute-start.21 = (f32[64,8,128]{2,1,0:T(8,128)S(1)}, f32[64,8,128]{2,1,0:T(8,128)S(1)}, u32[]{:S(2)}, u32[]{:S(2)}) collective-permute-start(f32[64,8,128]{2,1,0:T(8,128)S(1)} %get-tuple-element.108), channel_id=1, source_target_pairs={{0,7},{1,0},{2,1},{3,2},{4,3},{5,4},{6,5},{7,6},{8,15},{9,8},{10,9... | collective-permute-start | bytes 786440 | tf_op jit(solution)/shard_map/ppermute | solution.py:37
  50.0 1.2 %collective-permute-start.14 = (f32[65,8,128]{2,1,0:T(8,128)S(1)}, f32[65,8,128]{2,1,0:T(8,128)S(1)}, u32[]{:S(2)}, u32[]{:S(2)}) collective-permute-start(f32[65,8,128]{2,1,0:T(8,128)S(1)} %get-tuple-element.78), channel_id=1, source_target_pairs={{0,24},{1,25},{2,26},{3,27},{4,28},{5,29},{6,30},{7,31},{8,0},{9,1... | collective-permute-start | bytes 798728 | tf_op jit(solution)/shard_map/ppermute | solution.py:33
  51.2 5.2 %collective-permute-done.8.refs_2_ = f32[65,8,128]{2,1,0:T(8,128)S(1)} collective-permute-done((f32[65,8,128]{2,1,0:T(8,128)S(1)}, f32[65,8,128]{2,1,0:T(8,128)S(1)}, u32[]{:S(2)}, u32[]{:S(2)}) %collective-permute-start.8) | collective-permute-done | bytes 266272 | tf_op jit(solution)/shard_map/ppermute | solution.py:33
  57.1 1.4 %collective-permute-start.4 = (f32[65,8,128]{2,1,0:T(8,128)S(1)}, f32[65,8,128]{2,1,0:T(8,128)S(1)}, u32[]{:S(2)}, u32[]{:S(2)}) collective-permute-start(f32[65,8,128]{2,1,0:T(8,128)S(1)} %get-tuple-element.60), channel_id=1, source_target_pairs={{0,8},{1,9},{2,10},{3,11},{4,12},{5,13},{6,14},{7,15},{8,16},{9,17... | collective-permute-start | bytes 798728 | tf_op jit(solution)/shard_map/ppermute | solution.py:33
  58.5 2.0 %shard_map.69 = f32[264,8,128]{2,1,0:T(8,128)S(1)} custom-call(f32[65,8,128]{2,1,0:T(8,128)S(1)} %get-tuple-element.91.refs_0_, f32[65,8,128]{2,1,0:T(8,128)S(1)} %collective-permute-done.3.refs_1_, f32[65,8,128]{2,1,0:T(8,128)S(1)} %collective-permute-done.8.refs_2_, f32[65,8,128]{2,1,0:T(8,128)S(1)} %collective-permute-done.13.refs_3_), custom_call_target="tpu_custom_call" | custom-call | flops 4294967296 | bytes 1048576 | tf_op jit(solution)/shard_map/pallas_call | solution.py:293
  60.7 4.5 %collective-permute-start.22 = (f32[128,8,128]{2,1,0:T(8,128)S(1)}, f32[128,8,128]{2,1,0:T(8,128)S(1)}, u32[]{:S(2)}, u32[]{:S(2)}) collective-permute-start(f32[128,8,128]{2,1,0:T(8,128)S(1)} %get-tuple-element.106), channel_id=1, source_target_pairs={{0,7},{1,0},{2,1},{3,2},{4,3},{5,4},{6,5},{7,6},{8,15},{9,8},{10,9... | collective-permute-start | bytes 1572872 | tf_op jit(solution)/shard_map/ppermute | solution.py:37
  65.3 0.9 collective-permute-start.15
  66.2 1.5 %collective-permute-start.10 = (f32[65,8,128]{2,1,0:T(8,128)S(1)}, f32[65,8,128]{2,1,0:T(8,128)S(1)}, u32[]{:S(2)}, u32[]{:S(2)}) collective-permute-start(f32[65,8,128]{2,1,0:T(8,128)S(1)} %get-tuple-element.71), channel_id=1, source_target_pairs={{0,16},{1,17},{2,18},{3,19},{4,20},{5,21},{6,22},{7,23},{8,24},{9,... | collective-permute-start | bytes 798728 | tf_op jit(solution)/shard_map/ppermute | solution.py:33
  67.8 2.5 %collective-permute-start.5 = (f32[65,8,128]{2,1,0:T(8,128)S(1)}, f32[65,8,128]{2,1,0:T(8,128)S(1)}, u32[]{:S(2)}, u32[]{:S(2)}) collective-permute-start(f32[65,8,128]{2,1,0:T(8,128)S(1)} %get-tuple-element.62), channel_id=1, source_target_pairs={{0,8},{1,9},{2,10},{3,11},{4,12},{5,13},{6,14},{7,15},{8,16},{9,17... | collective-permute-start | bytes 798728 | tf_op jit(solution)/shard_map/ppermute | solution.py:33
  70.3 2.0 %shard_map.68 = f32[264,8,128]{2,1,0:T(8,128)S(1)} custom-call(f32[65,8,128]{2,1,0:T(8,128)S(1)} %get-tuple-element.87.refs_0_, f32[65,8,128]{2,1,0:T(8,128)S(1)} %collective-permute-done.4.refs_1_, f32[65,8,128]{2,1,0:T(8,128)S(1)} %collective-permute-done.9.refs_2_, f32[65,8,128]{2,1,0:T(8,128)S(1)} %collective-permute-done.14.refs_3_), custom_call_target="tpu_custom_call" | custom-call | flops 4294967296 | bytes 1048576 | tf_op jit(solution)/shard_map/pallas_call | solution.py:293
  72.3 3.7 %collective-permute-done.18 = f32[128,8,128]{2,1,0:T(8,128)S(1)} collective-permute-done((f32[128,8,128]{2,1,0:T(8,128)S(1)}, f32[128,8,128]{2,1,0:T(8,128)S(1)}, u32[]{:S(2)}, u32[]{:S(2)}) %collective-permute-start.18) | collective-permute-done | bytes 524320 | tf_op jit(solution)/shard_map/ppermute | solution.py:37
  76.6 2.9 %collective-permute-start.23 = (f32[128,8,128]{2,1,0:T(8,128)S(1)}, f32[128,8,128]{2,1,0:T(8,128)S(1)}, u32[]{:S(2)}, u32[]{:S(2)}) collective-permute-start(f32[128,8,128]{2,1,0:T(8,128)S(1)} %get-tuple-element.104), channel_id=1, source_target_pairs={{0,7},{1,0},{2,1},{3,2},{4,3},{5,4},{6,5},{7,6},{8,15},{9,8},{10,9... | collective-permute-start | bytes 1572872 | tf_op jit(solution)/shard_map/ppermute | solution.py:37
  79.6 1.8 %collective-permute-start.11 = (f32[33,8,128]{2,1,0:T(8,128)S(1)}, f32[33,8,128]{2,1,0:T(8,128)S(1)}, u32[]{:S(2)}, u32[]{:S(2)}) collective-permute-start(f32[33,8,128]{2,1,0:T(8,128)S(1)} %get-tuple-element.73), channel_id=1, source_target_pairs={{0,16},{1,17},{2,18},{3,19},{4,20},{5,21},{6,22},{7,23},{8,24},{9,... | collective-permute-start | bytes 405512 | tf_op jit(solution)/shard_map/ppermute | solution.py:33
  81.4 1.8 %collective-permute-start.6 = (f32[33,8,128]{2,1,0:T(8,128)S(1)}, f32[33,8,128]{2,1,0:T(8,128)S(1)}, u32[]{:S(2)}, u32[]{:S(2)}) collective-permute-start(f32[33,8,128]{2,1,0:T(8,128)S(1)} %get-tuple-element.64), channel_id=1, source_target_pairs={{0,8},{1,9},{2,10},{3,11},{4,12},{5,13},{6,14},{7,15},{8,16},{9,17... | collective-permute-start | bytes 405512 | tf_op jit(solution)/shard_map/ppermute | solution.py:33
  83.2 2.0 %shard_map.67 = f32[264,8,128]{2,1,0:T(8,128)S(1)} custom-call(f32[65,8,128]{2,1,0:T(8,128)S(1)} %get-tuple-element.83.refs_0_, f32[65,8,128]{2,1,0:T(8,128)S(1)} %collective-permute-done.5.refs_1_, f32[65,8,128]{2,1,0:T(8,128)S(1)} %collective-permute-done.10.refs_2_, f32[65,8,128]{2,1,0:T(8,128)S(1)} %collective-permute-done.15.refs_3_), custom_call_target="tpu_custom_call" | custom-call | flops 4294967296 | bytes 1048576 | tf_op jit(solution)/shard_map/pallas_call | solution.py:293
  85.2 4.3 %collective-permute-done.19 = f32[128,8,128]{2,1,0:T(8,128)S(1)} collective-permute-done((f32[128,8,128]{2,1,0:T(8,128)S(1)}, f32[128,8,128]{2,1,0:T(8,128)S(1)}, u32[]{:S(2)}, u32[]{:S(2)}) %collective-permute-start.19) | collective-permute-done | bytes 524320 | tf_op jit(solution)/shard_map/ppermute | solution.py:37
  89.8 3.2 %collective-permute-start.24 = (f32[128,8,128]{2,1,0:T(8,128)S(1)}, f32[128,8,128]{2,1,0:T(8,128)S(1)}, u32[]{:S(2)}, u32[]{:S(2)}) collective-permute-start(f32[128,8,128]{2,1,0:T(8,128)S(1)} %get-tuple-element.102), channel_id=1, source_target_pairs={{0,7},{1,0},{2,1},{3,2},{4,3},{5,4},{6,5},{7,6},{8,15},{9,8},{10,9... | collective-permute-start | bytes 1572872 | tf_op jit(solution)/shard_map/ppermute | solution.py:37
  93.0 1.3 %shard_map.66 = f32[264,8,128]{2,1,0:T(8,128)S(1)} custom-call(f32[33,8,128]{2,1,0:T(8,128)S(1)} %get-tuple-element.55.refs_0_, f32[33,8,128]{2,1,0:T(8,128)S(1)} %collective-permute-done.6.refs_1_, f32[33,8,128]{2,1,0:T(8,128)S(1)} %collective-permute-done.11.refs_2_, f32[33,8,128]{2,1,0:T(8,128)S(1)} %collective-permute-done.16.refs_3_), custom_call_target="tpu_custom_call" | custom-call | flops 4294967296 | bytes 1048576 | tf_op jit(solution)/shard_map/pallas_call | solution.py:293
  94.4 7.7 %collective-permute-done.20 = f32[128,8,128]{2,1,0:T(8,128)S(1)} collective-permute-done((f32[128,8,128]{2,1,0:T(8,128)S(1)}, f32[128,8,128]{2,1,0:T(8,128)S(1)}, u32[]{:S(2)}, u32[]{:S(2)}) %collective-permute-start.20) | collective-permute-done | bytes 524320 | tf_op jit(solution)/shard_map/ppermute | solution.py:37
  102.0 1.0 fusion.1
  (49 shorter events, 4.7 us)
Async XLA Ops:
  1.1 7.8 %collective-permute-start = (f32[8,1024]{1,0:T(8,128)S(1)}, f32[8,1024]{1,0:T(8,128)S(1)}, u32[]{:S(2)}, u32[]{:S(2)}) collective-permute-start(f32[8,1024]{1,0:T(8,128)S(1)} %bitcast.9), channel_id=1, source_target_pairs={{0,1},{1,2},{2,3},{3,4},{4,5},{5,6},{6,7},{7,8},{8,9},{9,10},{10,1... | collective-permute-start | bytes 98312 | tf_op jit(solution)/shard_map/ppermute | solution.py:312
  3.1 5.8 %collective-permute-start.1 = (f32[8,1024]{1,0:T(8,128)S(1)}, f32[8,1024]{1,0:T(8,128)S(1)}, u32[]{:S(2)}, u32[]{:S(2)}) collective-permute-start(f32[8,1024]{1,0:T(8,128)S(1)} %bitcast.10), channel_id=1, source_target_pairs={{1,0},{2,1},{3,2},{4,3},{5,4},{6,5},{7,6},{8,7},{9,8},{10,9},{11,1... | collective-permute-start | bytes 98312 | tf_op jit(solution)/shard_map/ppermute | solution.py:313
  8.9 0.6 copy-start.4
  8.9 0.6 copy-start.5
  22.7 17.3 %collective-permute-start.12 = (f32[33,8,128]{2,1,0:T(8,128)}, f32[33,8,128]{2,1,0:T(8,128)S(1)}, u32[]{:S(2)}, u32[]{:S(2)}) collective-permute-start(f32[33,8,128]{2,1,0:T(8,128)} %get-tuple-element.74), channel_id=1, source_target_pairs={{0,24},{1,25},{2,26},{3,27},{4,28},{5,29},{6,30},{7,31},{8,0},{9,1... | collective-permute-start | bytes 405512 | tf_op jit(solution)/shard_map/ppermute | solution.py:33
  25.3 14.8 %collective-permute-start.7 = (f32[33,8,128]{2,1,0:T(8,128)}, f32[33,8,128]{2,1,0:T(8,128)S(1)}, u32[]{:S(2)}, u32[]{:S(2)}) collective-permute-start(f32[33,8,128]{2,1,0:T(8,128)} %get-tuple-element.65), channel_id=1, source_target_pairs={{0,16},{1,17},{2,18},{3,19},{4,20},{5,21},{6,22},{7,23},{8,24},{9,... | collective-permute-start | bytes 405512 | tf_op jit(solution)/shard_map/ppermute | solution.py:33
  25.5 17.9 %collective-permute-start.2 = (f32[33,8,128]{2,1,0:T(8,128)}, f32[33,8,128]{2,1,0:T(8,128)S(1)}, u32[]{:S(2)}, u32[]{:S(2)}) collective-permute-start(f32[33,8,128]{2,1,0:T(8,128)} %get-tuple-element.56), channel_id=1, source_target_pairs={{0,8},{1,9},{2,10},{3,11},{4,12},{5,13},{6,14},{7,15},{8,16},{9,17... | collective-permute-start | bytes 405512 | tf_op jit(solution)/shard_map/ppermute | solution.py:33
  27.6 1.6 %copy-start = (f32[512,8,128]{2,1,0:T(8,128)S(1)}, f32[512,8,128]{2,1,0:T(8,128)}, u32[]{:S(2)}) copy-start(f32[512,8,128]{2,1,0:T(8,128)} %get-tuple-element.54.smooth) | copy-start | bytes 6291460
  29.2 0.7 copy-start.1
  29.9 0.6 copy-start.2
  30.5 13.6 %copy-start.3 = (f32[33,8,128]{2,1,0:T(8,128)S(1)}, f32[33,8,128]{2,1,0:T(8,128)}, u32[]{:S(2)}) copy-start(f32[33,8,128]{2,1,0:T(8,128)} %get-tuple-element.95.refs_0_) | copy-start | bytes 405508
  40.0 10.0 %collective-permute-start.13 = (f32[65,8,128]{2,1,0:T(8,128)S(1)}, f32[65,8,128]{2,1,0:T(8,128)S(1)}, u32[]{:S(2)}, u32[]{:S(2)}) collective-permute-start(f32[65,8,128]{2,1,0:T(8,128)S(1)} %get-tuple-element.76), channel_id=1, source_target_pairs={{0,24},{1,25},{2,26},{3,27},{4,28},{5,29},{6,30},{7,31},{8,0},{9,1... | collective-permute-start | bytes 798728 | tf_op jit(solution)/shard_map/ppermute | solution.py:33
  40.1 16.3 %collective-permute-start.8 = (f32[65,8,128]{2,1,0:T(8,128)S(1)}, f32[65,8,128]{2,1,0:T(8,128)S(1)}, u32[]{:S(2)}, u32[]{:S(2)}) collective-permute-start(f32[65,8,128]{2,1,0:T(8,128)S(1)} %get-tuple-element.67), channel_id=1, source_target_pairs={{0,16},{1,17},{2,18},{3,19},{4,20},{5,21},{6,22},{7,23},{8,24},{9,... | collective-permute-start | bytes 798728 | tf_op jit(solution)/shard_map/ppermute | solution.py:33
  43.4 13.7 %collective-permute-start.3 = (f32[65,8,128]{2,1,0:T(8,128)S(1)}, f32[65,8,128]{2,1,0:T(8,128)S(1)}, u32[]{:S(2)}, u32[]{:S(2)}) collective-permute-start(f32[65,8,128]{2,1,0:T(8,128)S(1)} %get-tuple-element.58), channel_id=1, source_target_pairs={{0,8},{1,9},{2,10},{3,11},{4,12},{5,13},{6,14},{7,15},{8,16},{9,17... | collective-permute-start | bytes 798728 | tf_op jit(solution)/shard_map/ppermute | solution.py:33
  45.5 15.0 %collective-permute-start.17 = (f32[64,8,128]{2,1,0:T(8,128)S(1)}, f32[64,8,128]{2,1,0:T(8,128)S(1)}, u32[]{:S(2)}, u32[]{:S(2)}) collective-permute-start(f32[64,8,128]{2,1,0:T(8,128)S(1)} %get-tuple-element.107), channel_id=1, source_target_pairs={{0,1},{1,2},{2,3},{3,4},{4,5},{5,6},{6,7},{7,0},{8,9},{9,10},{10,1... | collective-permute-start | bytes 786440 | tf_op jit(solution)/shard_map/ppermute | solution.py:37
  45.7 14.9 %collective-permute-start.21 = (f32[64,8,128]{2,1,0:T(8,128)S(1)}, f32[64,8,128]{2,1,0:T(8,128)S(1)}, u32[]{:S(2)}, u32[]{:S(2)}) collective-permute-start(f32[64,8,128]{2,1,0:T(8,128)S(1)} %get-tuple-element.108), channel_id=1, source_target_pairs={{0,7},{1,0},{2,1},{3,2},{4,3},{5,4},{6,5},{7,6},{8,15},{9,8},{10,9... | collective-permute-start | bytes 786440 | tf_op jit(solution)/shard_map/ppermute | solution.py:37
  50.0 15.2 %collective-permute-start.14 = (f32[65,8,128]{2,1,0:T(8,128)S(1)}, f32[65,8,128]{2,1,0:T(8,128)S(1)}, u32[]{:S(2)}, u32[]{:S(2)}) collective-permute-start(f32[65,8,128]{2,1,0:T(8,128)S(1)} %get-tuple-element.78), channel_id=1, source_target_pairs={{0,24},{1,25},{2,26},{3,27},{4,28},{5,29},{6,30},{7,31},{8,0},{9,1... | collective-permute-start | bytes 798728 | tf_op jit(solution)/shard_map/ppermute | solution.py:33
  56.4 9.8 %collective-permute-start.9 = (f32[65,8,128]{2,1,0:T(8,128)S(1)}, f32[65,8,128]{2,1,0:T(8,128)S(1)}, u32[]{:S(2)}, u32[]{:S(2)}) collective-permute-start(f32[65,8,128]{2,1,0:T(8,128)S(1)} %get-tuple-element.69), channel_id=1, source_target_pairs={{0,16},{1,17},{2,18},{3,19},{4,20},{5,21},{6,22},{7,23},{8,24},{9,... | collective-permute-start | bytes 798728 | tf_op jit(solution)/shard_map/ppermute | solution.py:33
  57.1 10.6 %collective-permute-start.4 = (f32[65,8,128]{2,1,0:T(8,128)S(1)}, f32[65,8,128]{2,1,0:T(8,128)S(1)}, u32[]{:S(2)}, u32[]{:S(2)}) collective-permute-start(f32[65,8,128]{2,1,0:T(8,128)S(1)} %get-tuple-element.60), channel_id=1, source_target_pairs={{0,8},{1,9},{2,10},{3,11},{4,12},{5,13},{6,14},{7,15},{8,16},{9,17... | collective-permute-start | bytes 798728 | tf_op jit(solution)/shard_map/ppermute | solution.py:33
  60.7 15.4 %collective-permute-start.18 = (f32[128,8,128]{2,1,0:T(8,128)S(1)}, f32[128,8,128]{2,1,0:T(8,128)S(1)}, u32[]{:S(2)}, u32[]{:S(2)}) collective-permute-start(f32[128,8,128]{2,1,0:T(8,128)S(1)} %get-tuple-element.105), channel_id=1, source_target_pairs={{0,1},{1,2},{2,3},{3,4},{4,5},{5,6},{6,7},{7,0},{8,9},{9,10},{10,1... | collective-permute-start | bytes 1572872 | tf_op jit(solution)/shard_map/ppermute | solution.py:37
  60.7 15.3 %collective-permute-start.22 = (f32[128,8,128]{2,1,0:T(8,128)S(1)}, f32[128,8,128]{2,1,0:T(8,128)S(1)}, u32[]{:S(2)}, u32[]{:S(2)}) collective-permute-start(f32[128,8,128]{2,1,0:T(8,128)S(1)} %get-tuple-element.106), channel_id=1, source_target_pairs={{0,7},{1,0},{2,1},{3,2},{4,3},{5,4},{6,5},{7,6},{8,15},{9,8},{10,9... | collective-permute-start | bytes 1572872 | tf_op jit(solution)/shard_map/ppermute | solution.py:37
  65.3 14.3 %collective-permute-start.15 = (f32[65,8,128]{2,1,0:T(8,128)S(1)}, f32[65,8,128]{2,1,0:T(8,128)S(1)}, u32[]{:S(2)}, u32[]{:S(2)}) collective-permute-start(f32[65,8,128]{2,1,0:T(8,128)S(1)} %get-tuple-element.80), channel_id=1, source_target_pairs={{0,24},{1,25},{2,26},{3,27},{4,28},{5,29},{6,30},{7,31},{8,0},{9,1... | collective-permute-start | bytes 798728 | tf_op jit(solution)/shard_map/ppermute | solution.py:33
  66.2 13.4 %collective-permute-start.10 = (f32[65,8,128]{2,1,0:T(8,128)S(1)}, f32[65,8,128]{2,1,0:T(8,128)S(1)}, u32[]{:S(2)}, u32[]{:S(2)}) collective-permute-start(f32[65,8,128]{2,1,0:T(8,128)S(1)} %get-tuple-element.71), channel_id=1, source_target_pairs={{0,16},{1,17},{2,18},{3,19},{4,20},{5,21},{6,22},{7,23},{8,24},{9,... | collective-permute-start | bytes 798728 | tf_op jit(solution)/shard_map/ppermute | solution.py:33
  67.8 13.6 %collective-permute-start.5 = (f32[65,8,128]{2,1,0:T(8,128)S(1)}, f32[65,8,128]{2,1,0:T(8,128)S(1)}, u32[]{:S(2)}, u32[]{:S(2)}) collective-permute-start(f32[65,8,128]{2,1,0:T(8,128)S(1)} %get-tuple-element.62), channel_id=1, source_target_pairs={{0,8},{1,9},{2,10},{3,11},{4,12},{5,13},{6,14},{7,15},{8,16},{9,17... | collective-permute-start | bytes 798728 | tf_op jit(solution)/shard_map/ppermute | solution.py:33
  76.2 13.3 %collective-permute-start.19 = (f32[128,8,128]{2,1,0:T(8,128)S(1)}, f32[128,8,128]{2,1,0:T(8,128)S(1)}, u32[]{:S(2)}, u32[]{:S(2)}) collective-permute-start(f32[128,8,128]{2,1,0:T(8,128)S(1)} %get-tuple-element.103), channel_id=1, source_target_pairs={{0,1},{1,2},{2,3},{3,4},{4,5},{5,6},{6,7},{7,0},{8,9},{9,10},{10,1... | collective-permute-start | bytes 1572872 | tf_op jit(solution)/shard_map/ppermute | solution.py:37
  76.6 12.9 %collective-permute-start.23 = (f32[128,8,128]{2,1,0:T(8,128)S(1)}, f32[128,8,128]{2,1,0:T(8,128)S(1)}, u32[]{:S(2)}, u32[]{:S(2)}) collective-permute-start(f32[128,8,128]{2,1,0:T(8,128)S(1)} %get-tuple-element.104), channel_id=1, source_target_pairs={{0,7},{1,0},{2,1},{3,2},{4,3},{5,4},{6,5},{7,6},{8,15},{9,8},{10,9... | collective-permute-start | bytes 1572872 | tf_op jit(solution)/shard_map/ppermute | solution.py:37
  79.6 13.4 %collective-permute-start.16 = (f32[33,8,128]{2,1,0:T(8,128)S(1)}, f32[33,8,128]{2,1,0:T(8,128)S(1)}, u32[]{:S(2)}, u32[]{:S(2)}) collective-permute-start(f32[33,8,128]{2,1,0:T(8,128)S(1)} %get-tuple-element.82), channel_id=1, source_target_pairs={{0,24},{1,25},{2,26},{3,27},{4,28},{5,29},{6,30},{7,31},{8,0},{9,1... | collective-permute-start | bytes 405512 | tf_op jit(solution)/shard_map/ppermute | solution.py:33
  79.6 13.4 %collective-permute-start.11 = (f32[33,8,128]{2,1,0:T(8,128)S(1)}, f32[33,8,128]{2,1,0:T(8,128)S(1)}, u32[]{:S(2)}, u32[]{:S(2)}) collective-permute-start(f32[33,8,128]{2,1,0:T(8,128)S(1)} %get-tuple-element.73), channel_id=1, source_target_pairs={{0,16},{1,17},{2,18},{3,19},{4,20},{5,21},{6,22},{7,23},{8,24},{9,... | collective-permute-start | bytes 405512 | tf_op jit(solution)/shard_map/ppermute | solution.py:33
  81.4 11.6 %collective-permute-start.6 = (f32[33,8,128]{2,1,0:T(8,128)S(1)}, f32[33,8,128]{2,1,0:T(8,128)S(1)}, u32[]{:S(2)}, u32[]{:S(2)}) collective-permute-start(f32[33,8,128]{2,1,0:T(8,128)S(1)} %get-tuple-element.64), channel_id=1, source_target_pairs={{0,8},{1,9},{2,10},{3,11},{4,12},{5,13},{6,14},{7,15},{8,16},{9,17... | collective-permute-start | bytes 405512 | tf_op jit(solution)/shard_map/ppermute | solution.py:33
  85.2 7.8 %copy-start.6 = (s32[128]{0:T(128)S(1)}, s32[128]{0:T(128)}, u32[]{:S(2)}) copy-start(s32[128]{0:T(128)} %param.11) | copy-start | bytes 1540
  89.7 12.3 %collective-permute-start.20 = (f32[128,8,128]{2,1,0:T(8,128)S(1)}, f32[128,8,128]{2,1,0:T(8,128)S(1)}, u32[]{:S(2)}, u32[]{:S(2)}) collective-permute-start(f32[128,8,128]{2,1,0:T(8,128)S(1)} %get-tuple-element.101), channel_id=1, source_target_pairs={{0,1},{1,2},{2,3},{3,4},{4,5},{5,6},{6,7},{7,0},{8,9},{9,10},{10,1... | collective-permute-start | bytes 1572872 | tf_op jit(solution)/shard_map/ppermute | solution.py:37
  89.8 12.3 %collective-permute-start.24 = (f32[128,8,128]{2,1,0:T(8,128)S(1)}, f32[128,8,128]{2,1,0:T(8,128)S(1)}, u32[]{:S(2)}, u32[]{:S(2)}) collective-permute-start(f32[128,8,128]{2,1,0:T(8,128)S(1)} %get-tuple-element.102), channel_id=1, source_target_pairs={{0,7},{1,0},{2,1},{3,2},{4,3},{5,4},{6,5},{7,6},{8,15},{9,8},{10,9... | collective-permute-start | bytes 1572872 | tf_op jit(solution)/shard_map/ppermute | solution.py:37

commit v2 on v1

--- a/solution.py
+++ b/solution.py
@@ -15,11 +15,14 @@
 GROUP = 16
 PART = 32
 WEIGHT_PARTS = PAIRS // PART
-FAR_VMEM, NEAR_VMEM = 56, 48
+FAR_VMEM, NEAR_VMEM = 44, 44
 DISTANCES = (4, 3, 2, 1, 0)
 SIZES = (CAP, 2 * CAP, 2 * CAP, 2 * CAP, CAP)
 STARTS = tuple(X * (sum(SIZES[:n]) + n) for n in range(len(SIZES) + 1))
 BITS = 9
+MESSAGES = X * len(SIZES)
+META_ROWS = 1 + MESSAGES // 4
+FAR = 2
 LAND_BITS = 12
 
 
@@ -37,7 +40,7 @@
     return lax.ppermute(a, "tile", shift(0, dz))
 
 
-def make_plan(packed, jobs_ref, order_ref, bounds_ref, table_ref):
+def make_plan(packed, meta_ref, order_ref, bounds_ref, table_ref):
     land, atm = packed & ((1 << LAND_BITS) - 1), packed >> LAND_BITS
     t = lax.axis_index("tile")
     x, z = t // Z, t % Z
@@ -48,7 +51,7 @@
     start = jnp.zeros_like(dist)
     for n, d in enumerate(DISTANCES):
         start = jnp.where(dist == d, STARTS[n] + ex * (SIZES[n] + 1), start)
-    bounds_ref[0] = jnp.sum((start < STARTS[1]).astype(jnp.int32))
+    bounds_ref[0] = jnp.sum((start < STARTS[FAR]).astype(jnp.int32))
     target = row + jnp.where(delta > 4, LAND, 0) - EMPTY
 
     def column(a):
@@ -69,7 +72,7 @@
     place = rank + total(jnp.where(start_col < start, one, nil))
     slot = start + rank
     job = p_row + (atm << BITS) + (slot << (2 * BITS))
-    jobs_ref[...] = job
+    meta_ref[0:1] = job
     order_ref[...] = total(jnp.where(column(place) == p_row, column(job), 0))
     slot_col, target_col = column(slot), column(target)
     lane = lax.broadcasted_iota(jnp.int32, (1, B), 1)
@@ -79,8 +82,17 @@
             spot = jnp.where(lane < B // 2, head + lane, head + SIZES[n] + 1 + lane - B // 2)
             spot = jnp.where(lane % (B // 2) < SIZES[n], spot, -1)
             hit = total(jnp.where(slot_col == spot, target_col, 0))
+            used = (hit != 0).astype(jnp.int32)
+            left = jnp.sum(jnp.where(lane < B // 2, used, 0), axis=1, keepdims=True)
+            right = jnp.sum(used, axis=1, keepdims=True) - left
             k = n * (X // 2) + m
-            table_ref[k : k + 1] = (EMPTY + hit).astype(jnp.float32)
+            table_ref[k : k + 1] = EMPTY + hit
+            table_ref[MESSAGES // 2 + k : MESSAGES // 2 + k + 1] = jnp.where(
+                lane < B // 2, left, right
+            )
+    for k in range(MESSAGES):
+        at = slice(k % 4 * B, (k % 4 + 1) * B)
+        meta_ref[1 + k // 4 : 2 + k // 4, at] = table_ref[k : k + 1]
 
 
 def start_weights(w_ref, w, sem):
@@ -94,12 +106,23 @@
     pltpu.make_async_copy(w_ref.at[at], w.at[at], sem.at[n]).wait()
 
 
-def put_targets(table, send, first, last, base):
+def put_targets(row, send, first, last, base):
     for n in range(first, last):
         for e in range(X):
             end = STARTS[n] + (e + 1) * (SIZES[n] + 1) - 1 - base
             k = n * (X // 2) + e // 2
-            send[end, 0:1] = table[k : k + 1]
+            send[end, 0:1] = row(k).astype(jnp.float32)
+            send[end, 1:2] = row(MESSAGES // 2 + k).astype(jnp.float32)
+
+
+def multiply_two(left, right, w):
+    left, right = left.astype(jnp.bfloat16), right.astype(jnp.bfloat16)
+    nil = jnp.zeros_like(left)
+    both = jnp.concatenate(
+        [jnp.concatenate([left, nil], axis=1), jnp.concatenate([nil, right], axis=1)], axis=0
+    )
+    out = jnp.dot(both, w, preferred_element_type=jnp.float32)
+    return out[:F], out[F:]
 
 
 def put_messages(send, outs, sem, first, last, base):
@@ -117,10 +140,9 @@
         c.wait()
 
 
-def far_kernel(
-    atmos, kappa, packed, north, south, w_ref, smooth, jobs, table, *rest
-):
-    *outs, field, coeff, pairs, edge, rows, order, place, bounds, w, send, w_sem, out_sem, sem = rest
+def far_kernel(atmos, kappa, packed, north, south, w_ref, smooth, meta, *rest):
+    *outs, field, coeff, pairs, edge, rows, order, table, place, bounds, w, send = rest[:-3]
+    w_sem, out_sem, sem = rest[-3:]
     per = COLS // B
     small = pltpu.make_async_copy(packed, pairs, sem.at[per])
     small.start()
@@ -134,13 +156,13 @@
     ]
     for c in copies:
         c.start()
+    small.wait()
+    for c in copies:
+        c.wait()
     start_weights(w_ref, w, w_sem)
-    small.wait()
-    make_plan(pairs[...], jobs, order, bounds, table)
+    make_plan(pairs[...], meta, order, bounds, table)
     to_smem = pltpu.make_async_copy(order, place, sem.at[per])
     to_smem.start()
-    for c in copies:
-        c.wait()
     tile = lax.axis_index("tile")
     above = jnp.where(tile > 0, edge[0], 0.0)
     under = jnp.where(tile < X * Z - 1, edge[1], 0.0)
@@ -162,7 +184,7 @@
     lax.fori_loop(0, ROWS, step, (above, row(0)), unroll=2)
     save = pltpu.make_async_copy(rows, smooth, sem.at[0])
     save.start()
-    put_targets(table, send, 0, 1, 0)
+    put_targets(lambda k: table[k : k + 1], send, 0, FAR, 0)
     to_smem.wait()
     for n in range(WEIGHT_PARTS):
         wait_weights(w_ref, w, w_sem, n)
@@ -170,42 +192,56 @@
     high = bounds[0]
 
     def multiply(n, carry):
-        for j in range(GROUP):
-            job = place[0, jnp.minimum(n * GROUP + j, high - 1)]
-            block = rows[(job >> BITS) & mask].astype(jnp.bfloat16)
-            send[job >> (2 * BITS)] = jnp.dot(
-                block, w[job & mask], preferred_element_type=jnp.float32
+        for j in range(0, GROUP, 2):
+            one = place[0, jnp.minimum(n * GROUP + j, high - 1)]
+            two = place[0, jnp.minimum(n * GROUP + j + 1, high - 1)]
+            send[one >> (2 * BITS)], send[two >> (2 * BITS)] = multiply_two(
+                rows[(one >> BITS) & mask],
+                rows[(two >> BITS) & mask],
+                jnp.concatenate([w[one & mask], w[two & mask]], axis=0),
             )
         return carry
 
     lax.fori_loop(0, (high + GROUP - 1) // GROUP, multiply, 0)
-    put_messages(send, outs, out_sem, 0, 1, 0)
+    put_messages(send, outs, out_sem, 0, FAR, 0)
     save.wait()
 
 
-def near_kernel(jobs, table, smooth, w_ref, *rest):
-    *outs, rows, w, send, w_sem, out_sem, sem = rest
-    base = STARTS[1] - 1
+def near_kernel(meta, smooth, w_ref, *rest):
+    *outs, info, jobs, rows, w, send, w_sem, out_sem, sem = rest
+    base = STARTS[FAR] - 1
+    loads = [
+        pltpu.make_async_copy(meta, info, sem.at[0]),
+        pltpu.make_async_copy(meta.at[pl.ds(0, 1)], jobs, sem.at[1]),
+        pltpu.make_async_copy(smooth, rows, sem.at[2]),
+    ]
+    for c in loads:
+        c.start()
     start_weights(w_ref, w, w_sem)
-    load = pltpu.make_async_copy(smooth, rows, sem)
-    load.start()
-    put_targets(table, send, 1, len(SIZES), base)
-    load.wait()
+    for c in loads:
+        c.wait()
+    put_targets(
+        lambda k: info[1 + k // 4 : 2 + k // 4, k % 4 * B : (k % 4 + 1) * B],
+        send, FAR, len(SIZES), base,
+    )
     mask = (1 << BITS) - 1
 
     def multiply(n, carry):
         wait_weights(w_ref, w, w_sem, n)
-        for j in range(PART):
+        for j in range(0, PART, 2):
             p = n * PART + j
-            job = jobs[0, p]
-            block = rows[(job >> BITS) & mask].astype(jnp.bfloat16)
-            send[jnp.maximum((job >> (2 * BITS)) - base, 0)] = jnp.dot(
-                block, w[p], preferred_element_type=jnp.float32
+            one, two = jobs[0, p], jobs[0, p + 1]
+            to_one = jnp.maximum((one >> (2 * BITS)) - base, 0)
+            to_two = jnp.maximum((two >> (2 * BITS)) - base, 0)
+            send[to_one], send[to_two] = multiply_two(
+                rows[(one >> BITS) & mask],
+                rows[(two >> BITS) & mask],
+                w[pl.ds(p, 2)].reshape(2 * B, B),
             )
         return carry
 
     lax.fori_loop(0, WEIGHT_PARTS, multiply, 0)
-    put_messages(send, outs, out_sem, 1, len(SIZES), base)
+    put_messages(send, outs, out_sem, FAR, len(SIZES), base)
 
 
 def messages(first, last):
@@ -218,17 +254,16 @@
 
 def remap_far(atmos, kappa, packed, north, south, weights):
     vmem, anywhere = (pl.BlockSpec(memory_space=m) for m in (pltpu.VMEM, pl.ANY))
-    shapes = messages(0, 1)
-    smooth, jobs, table, *outs = pl.pallas_call(
+    shapes = messages(0, FAR)
+    smooth, meta, *outs = pl.pallas_call(
         far_kernel,
         out_shape=[
             jax.ShapeDtypeStruct((ROWS * COLS // B, F, B), jnp.float32),
-            jax.ShapeDtypeStruct((1, PAIRS), jnp.int32),
-            jax.ShapeDtypeStruct((len(SIZES) * X // 2, B), jnp.float32),
+            jax.ShapeDtypeStruct((META_ROWS, PAIRS), jnp.int32),
         ]
         + shapes,
         in_specs=[anywhere] * 6,
-        out_specs=[anywhere, vmem, vmem] + [anywhere] * len(shapes),
+        out_specs=[anywhere, vmem] + [anywhere] * len(shapes),
         scratch_shapes=[
             pltpu.VMEM((COLS // B, F * ROWS, B), jnp.float32),
             pltpu.VMEM((ROWS, COLS), jnp.float32),
@@ -236,10 +271,11 @@
             pltpu.VMEM((2, F, COLS), jnp.float32),
             pltpu.VMEM((ROWS * COLS // B, F, B), jnp.float32),
             pltpu.VMEM((1, PAIRS), jnp.int32),
+            pltpu.VMEM((MESSAGES, B), jnp.int32),
             pltpu.SMEM((1, PAIRS), jnp.int32),
             pltpu.SMEM((1,), jnp.int32),
             pltpu.VMEM((PAIRS, B, B), jnp.bfloat16),
-            pltpu.VMEM((STARTS[1], F, B), jnp.float32),
+            pltpu.VMEM((STARTS[FAR], F, B), jnp.float32),
             pltpu.SemaphoreType.DMA((WEIGHT_PARTS,)),
             pltpu.SemaphoreType.DMA((len(shapes),)),
             pltpu.SemaphoreType.DMA((COLS // B + 4,)),
@@ -247,46 +283,49 @@
         compiler_params=pltpu.CompilerParams(vmem_limit_bytes=FAR_VMEM << 20),
         cost_estimate=pl.CostEstimate(flops=1 << 20, bytes_accessed=20 << 20, transcendentals=0),
     )(atmos.reshape(F * ROWS, COLS), kappa, packed, north, south, weights)
-    return smooth, jobs, table, outs
-
-
-def remap_near(jobs, table, smooth, weights):
-    smem, vmem, anywhere = (
-        pl.BlockSpec(memory_space=m) for m in (pltpu.SMEM, pltpu.VMEM, pl.ANY)
-    )
-    shapes = messages(1, len(SIZES))
+    return smooth, meta, outs
+
+
+def remap_near(meta, smooth, weights):
+    shapes = messages(FAR, len(SIZES))
     return pl.pallas_call(
         near_kernel,
         out_shape=shapes,
-        in_specs=[smem, vmem, anywhere, anywhere],
-        out_specs=[anywhere] * len(shapes),
+        in_specs=[pl.BlockSpec(memory_space=pl.ANY)] * 3,
+        out_specs=[pl.BlockSpec(memory_space=pl.ANY)] * len(shapes),
         scratch_shapes=[
+            pltpu.VMEM((META_ROWS, PAIRS), jnp.int32),
+            pltpu.SMEM((1, PAIRS), jnp.int32),
             pltpu.VMEM((ROWS * COLS // B, F, B), jnp.float32),
             pltpu.VMEM((PAIRS, B, B), jnp.bfloat16),
-            pltpu.VMEM((STARTS[-1] - STARTS[1] + 1, F, B), jnp.float32),
+            pltpu.VMEM((STARTS[-1] - STARTS[FAR] + 1, F, B), jnp.float32),
             pltpu.SemaphoreType.DMA((WEIGHT_PARTS,)),
             pltpu.SemaphoreType.DMA((len(shapes),)),
-            pltpu.SemaphoreType.DMA,
+            pltpu.SemaphoreType.DMA((3,)),
         ],
         compiler_params=pltpu.CompilerParams(vmem_limit_bytes=NEAR_VMEM << 20),
-        cost_estimate=pl.CostEstimate(flops=1 << 20, bytes_accessed=24 << 20, transcendentals=0),
-    )(jobs, table, smooth, weights)
+        cost_estimate=pl.CostEstimate(flops=1 << 33, bytes_accessed=24 << 20, transcendentals=0),
+    )(meta, smooth, weights)
 
 
 def gather_kernel(size, a0, a1, a2, a3, out, wide, index, sem):
     for n, a in enumerate((a0, a1, a2, a3)):
         wide[n : n + 1] = a[size, 0:1].astype(jnp.int32)
+        wide[X + n : X + n + 1] = a[size, 1:2].astype(jnp.int32)
     copy = pltpu.make_async_copy(wide, index, sem)
     copy.start()
     out[...] = jnp.zeros_like(out)
     copy.wait()
     for n, a in enumerate((a0, a1, a2, a3)):
 
-        def add(s, carry, n=n, a=a):
-            out[index[n, s + (n % 2) * (B // 2)]] += a[s]
+        lane = (n % 2) * (B // 2)
+
+        def add(g, carry, n=n, a=a, lane=lane):
+            for j in range(8):
+                out[index[n, lane + g * 8 + j]] += a[g * 8 + j]
             return carry
 
-        lax.fori_loop(0, size, add, 0, unroll=8)
+        lax.fori_loop(0, (index[X + n, lane] + 7) // 8, add, 0)
 
 
 def gather_class(size, slots):
@@ -312,14 +351,15 @@
     north = lax.ppermute(atmos[:, -1, :], "tile", [(i, (i + 1) % tiles) for i in range(tiles)])
     south = lax.ppermute(atmos[:, 0, :], "tile", [((i + 1) % tiles, i) for i in range(tiles)])
     packed = (pair_land + (pair_atm << LAND_BITS)).reshape(1, PAIRS)
-    smooth, jobs, table, out = remap_far(atmos, kappa, packed, north, south, weights)
-    near = remap_near(jobs, table, smooth, weights)
-    sends = [out] + [near[n * X : (n + 1) * X] for n in range(len(SIZES) - 1)]
+    smooth, meta, far = remap_far(atmos, kappa, packed, north, south, weights)
+    sends = [*far, *remap_near(meta, smooth, weights)]
+    sends = [sends[n * X : (n + 1) * X] for n in range(len(SIZES))]
     dense = {}
     came = None
     for n, (own, *away) in enumerate(sends):
         if came is not None:
-            came, away = zip(*(lax.optimization_barrier(both) for both in zip(came, away)))
+            if n >= FAR:
+                came, away = zip(*(lax.optimization_barrier(both) for both in zip(came, away)))
             dense[DISTANCES[n - 1]] = gather_class(SIZES[n - 1], [mine, *came])
         came, mine = [send_x(a, ex + 1) for ex, a in enumerate(away)], own
     dense[0] = gather_class(SIZES[-1], [mine, *came])

time: 103 us -> 94.1 us (0.914)
  the two profiles are of different devices: /device:TPU:2 before, /device:TPU:6 now
where the time goes in v2:
time: 94.1 us; the launch traced here: 93.8 us
  starting transfers between devices  43.8 us (47%)
  Pallas kernels  23.5 us (25%)
  waiting for transfers between devices  20.6 us (22%)
  local copies, waits for them, and re-layouts  3.68 us (4%)
  other arithmetic  2.13 us (2%)
    ppermute x8, starting transfers between devices, send_z(): return lax.ppermute(a, 'tile', shift(0, dz))  19.4 us
    ppermute x15, starting transfers between devices, send_x(): return lax.ppermute(a, 'tile', shift(dx, 0))  18.1 us
    ppermute x8, waiting for transfers between devices, send_z(): return lax.ppermute(a, 'tile', shift(0, dz))  13.1 us
    pallas_call x1, Pallas kernels, remap_far(): pl.pallas_call(far_kernel, out_shape=[jax.ShapeDtypeStruct((ROWS * COLS /...  9.81 us
    pallas_call x1, Pallas kernels, remap_near(): pl.pallas_call(near_kernel, out_shape=shapes, in_specs=[pl.BlockSpec(memo...  7.52 us
    ppermute x15, waiting for transfers between devices, send_x(): return lax.ppermute(a, 'tile', shift(dx, 0))  6.44 us
    pallas_call x5, Pallas kernels, gather_class(): pl.pallas_call(lambda *refs: gather_kernel(size, *refs), out_shape=jax.Sh...  6.12 us
    ppermute x1, starting transfers between devices, body(): lax.ppermute(atmos[:, 0, :], 'tile', [((i + 1) % tiles, i) for i in range...  4.3 us
  transfers between devices with their start and end apart: 25, of which 8 were waited for; matrix products, arithmetic and copies ran while one was open for 1% of the time, Pallas kernels for 15%

profile of v2, /device:TPU:6, one launch (start us, length us, event | category | flops | bytes accessed | tf_op | source)
XLA Modules:
  0.0 93.8 jit_solution(3522336995628004757)
XLA Ops:
  0.0 1.1 %fusion.2 = (f32[8,1,1024]{2,1,0:T(1,128)S(1)}, f32[8,1,1024]{2,1,0:T(1,128)S(1)}) fusion(f32[8,64,1024]{2,1,0:T(8,128)} %param.6), kind=kLoop, calls=%fused_computation.12 | loop fusion | bytes 131072 | tf_op jit(solution)/shard_map/slice | solution.py:352
  1.1 2.0 %collective-permute-start = (f32[8,1024]{1,0:T(8,128)S(1)}, f32[8,1024]{1,0:T(8,128)S(1)}, u32[]{:S(2)}, u32[]{:S(2)}) collective-permute-start(f32[8,1024]{1,0:T(8,128)S(1)} %bitcast.10), channel_id=1, source_target_pairs={{0,1},{1,2},{2,3},{3,4},{4,5},{5,6},{6,7},{7,8},{8,9},{9,10},{10,1... | collective-permute-start | bytes 98312 | tf_op jit(solution)/shard_map/ppermute | solution.py:351
  3.1 4.3 %collective-permute-start.1 = (f32[8,1024]{1,0:T(8,128)S(1)}, f32[8,1024]{1,0:T(8,128)S(1)}, u32[]{:S(2)}, u32[]{:S(2)}) collective-permute-start(f32[8,1024]{1,0:T(8,128)S(1)} %bitcast.11), channel_id=1, source_target_pairs={{1,0},{2,1},{3,2},{4,3},{5,4},{6,5},{7,6},{8,7},{9,8},{10,9},{11,1... | collective-permute-start | bytes 98312 | tf_op jit(solution)/shard_map/ppermute | solution.py:352
  8.1 1.1 %collective-permute-done.north = f32[8,1024]{1,0:T(8,128)S(1)} collective-permute-done((f32[8,1024]{1,0:T(8,128)S(1)}, f32[8,1024]{1,0:T(8,128)S(1)}, u32[]{:S(2)}, u32[]{:S(2)}) %collective-permute-start) | collective-permute-done | bytes 32800 | tf_op jit(solution)/shard_map/ppermute | solution.py:351
  9.2 1.6 %copy-done = f32[8,64,1024]{2,1,0:T(8,128)S(1)} copy-done((f32[8,64,1024]{2,1,0:T(8,128)S(1)}, f32[8,64,1024]{2,1,0:T(8,128)}, u32[]{:S(2)}) %copy-start) | copy-done | bytes 2097176
  10.8 0.9 %copy-done.1 = f32[64,1024]{1,0:T(8,128)S(1)} copy-done((f32[64,1024]{1,0:T(8,128)S(1)}, f32[64,1024]{1,0:T(8,128)}, u32[]{:S(2)}) %copy-start.1) | copy-done | bytes 262168
  11.7 9.8 %shard_map.64 = (f32[512,8,128]{2,1,0:T(8,128)S(1)}, s32[6,512]{1,0:T(8,128)S(1)}, f32[33,8,128]{2,1,0:T(8,128)S(1)}, f32[33,8,128]{2,1,0:T(8,128)S(1)}, f32[33,...) custom-call(f32[512,1024]{1,0:T(8,128)S(1)} %bitcast.8, ...), custom_call_target="tpu_custom_call" | custom-call | flops 1048576 | bytes 20971520 | tf_op jit(solution)/shard_map/pallas_call | solution.py:258
  21.6 2.5 %collective-permute-start.14 = (f32[33,8,128]{2,1,0:T(8,128)S(1)}, f32[33,8,128]{2,1,0:T(8,128)S(1)}, u32[]{:S(2)}, u32[]{:S(2)}) collective-permute-start(f32[33,8,128]{2,1,0:T(8,128)S(1)} %get-tuple-element.82), channel_id=1, source_target_pairs={{0,8},{1,9},{2,10},{3,11},{4,12},{5,13},{6,14},{7,15},{8,16},{9,17... | collective-permute-start | bytes 405512 | tf_op jit(solution)/shard_map/ppermute | solution.py:36
  25.0 2.7 %collective-permute-start.2 = (f32[65,8,128]{2,1,0:T(8,128)S(1)}, f32[65,8,128]{2,1,0:T(8,128)S(1)}, u32[]{:S(2)}, u32[]{:S(2)}) collective-permute-start(f32[65,8,128]{2,1,0:T(8,128)S(1)} %get-tuple-element.48), channel_id=1, source_target_pairs={{0,8},{1,9},{2,10},{3,11},{4,12},{5,13},{6,14},{7,15},{8,16},{9,17... | collective-permute-start | bytes 798728 | tf_op jit(solution)/shard_map/ppermute | solution.py:36
  27.7 1.9 %collective-permute-start.6 = (f32[65,8,128]{2,1,0:T(8,128)S(1)}, f32[65,8,128]{2,1,0:T(8,128)S(1)}, u32[]{:S(2)}, u32[]{:S(2)}) collective-permute-start(f32[65,8,128]{2,1,0:T(8,128)S(1)} %get-tuple-element.55), channel_id=1, source_target_pairs={{0,16},{1,17},{2,18},{3,19},{4,20},{5,21},{6,22},{7,23},{8,24},{9,... | collective-permute-start | bytes 798728 | tf_op jit(solution)/shard_map/ppermute | solution.py:36
  29.6 7.5 %shard_map.65 = (f32[65,8,128]{2,1,0:T(8,128)S(1)}, f32[65,8,128]{2,1,0:T(8,128)S(1)}, f32[65,8,128]{2,1,0:T(8,128)S(1)}, f32[65,8,128]{2,1,0:T(8,128)S(1)}, f32...) custom-call(s32[6,512]{1,0:T(8,128)S(1)} %get-tuple-element.45.meta,, ...), custom_call_target="tpu_custom_call" | custom-call | flops 8589934592 | bytes 25165824 | tf_op jit(solution)/shard_map/pallas_call | solution.py:291
  37.3 1.1 %shard_map.70 = f32[264,8,128]{2,1,0:T(8,128)S(1)} custom-call(f32[33,8,128]{2,1,0:T(8,128)S(1)} %get-tuple-element.81.refs_0_, f32[33,8,128]{2,1,0:T(8,128)S(1)} %collective-permute-done.14.refs_1_, f32[33,8,128]{2,1,0:T(8,128)S(1)} %collective-permute-done.15.refs_2_, f32[33,8,128]{2,1,0:T(8,128)S(1)} %collective-permute-done.16.refs_3_), custom_call_target="tpu_custom_call" | custom-call | flops 4294967296 | bytes 1048576 | tf_op jit(solution)/shard_map/pallas_call | solution.py:332
  38.5 5.0 %collective-permute-start.21 = (f32[64,8,128]{2,1,0:T(8,128)S(1)}, f32[64,8,128]{2,1,0:T(8,128)S(1)}, u32[]{:S(2)}, u32[]{:S(2)}) collective-permute-start(f32[64,8,128]{2,1,0:T(8,128)S(1)} %get-tuple-element.94), channel_id=1, source_target_pairs={{0,7},{1,0},{2,1},{3,2},{4,3},{5,4},{6,5},{7,6},{8,15},{9,8},{10,9... | collective-permute-start | bytes 786440 | tf_op jit(solution)/shard_map/ppermute | solution.py:40
  43.5 1.4 %collective-permute-done.10.refs_3_ = f32[65,8,128]{2,1,0:T(8,128)S(1)} collective-permute-done((f32[65,8,128]{2,1,0:T(8,128)S(1)}, f32[65,8,128]{2,1,0:T(8,128)S(1)}, u32[]{:S(2)}, u32[]{:S(2)}) %collective-permute-start.10) | collective-permute-done | bytes 266272 | tf_op jit(solution)/shard_map/ppermute | solution.py:36
  44.8 2.0 %collective-permute-start.7 = (f32[65,8,128]{2,1,0:T(8,128)S(1)}, f32[65,8,128]{2,1,0:T(8,128)S(1)}, u32[]{:S(2)}, u32[]{:S(2)}) collective-permute-start(f32[65,8,128]{2,1,0:T(8,128)S(1)} %get-tuple-element.57), channel_id=1, source_target_pairs={{0,16},{1,17},{2,18},{3,19},{4,20},{5,21},{6,22},{7,23},{8,24},{9,... | collective-permute-start | bytes 798728 | tf_op jit(solution)/shard_map/ppermute | solution.py:36
  46.9 1.9 %collective-permute-start.3 = (f32[65,8,128]{2,1,0:T(8,128)S(1)}, f32[65,8,128]{2,1,0:T(8,128)S(1)}, u32[]{:S(2)}, u32[]{:S(2)}) collective-permute-start(f32[65,8,128]{2,1,0:T(8,128)S(1)} %get-tuple-element.50), channel_id=1, source_target_pairs={{0,8},{1,9},{2,10},{3,11},{4,12},{5,13},{6,14},{7,15},{8,16},{9,17... | collective-permute-start | bytes 798728 | tf_op jit(solution)/shard_map/ppermute | solution.py:36
  48.8 1.4 %shard_map.69 = f32[264,8,128]{2,1,0:T(8,128)S(1)} custom-call(f32[65,8,128]{2,1,0:T(8,128)S(1)} %get-tuple-element.77.refs_0_, f32[65,8,128]{2,1,0:T(8,128)S(1)} %collective-permute-done.2.refs_1_, f32[65,8,128]{2,1,0:T(8,128)S(1)} %collective-permute-done.6.refs_2_, f32[65,8,128]{2,1,0:T(8,128)S(1)} %collective-permute-done.10.refs_3_), custom_call_target="tpu_custom_call" | custom-call | flops 4294967296 | bytes 1048576 | tf_op jit(solution)/shard_map/pallas_call | solution.py:332
  50.5 3.9 %collective-permute-start.22 = (f32[128,8,128]{2,1,0:T(8,128)S(1)}, f32[128,8,128]{2,1,0:T(8,128)S(1)}, u32[]{:S(2)}, u32[]{:S(2)}) collective-permute-start(f32[128,8,128]{2,1,0:T(8,128)S(1)} %get-tuple-element.92), channel_id=1, source_target_pairs={{0,7},{1,0},{2,1},{3,2},{4,3},{5,4},{6,5},{7,6},{8,15},{9,8},{10,9... | collective-permute-start | bytes 1572872 | tf_op jit(solution)/shard_map/ppermute | solution.py:40
  54.5 4.9 %collective-permute-done.7.refs_2_ = f32[65,8,128]{2,1,0:T(8,128)S(1)} collective-permute-done((f32[65,8,128]{2,1,0:T(8,128)S(1)}, f32[65,8,128]{2,1,0:T(8,128)S(1)}, u32[]{:S(2)}, u32[]{:S(2)}) %collective-permute-start.7) | collective-permute-done | bytes 266272 | tf_op jit(solution)/shard_map/ppermute | solution.py:36
  59.9 2.4 %collective-permute-start.4 = (f32[65,8,128]{2,1,0:T(8,128)S(1)}, f32[65,8,128]{2,1,0:T(8,128)S(1)}, u32[]{:S(2)}, u32[]{:S(2)}) collective-permute-start(f32[65,8,128]{2,1,0:T(8,128)S(1)} %get-tuple-element.52), channel_id=1, source_target_pairs={{0,8},{1,9},{2,10},{3,11},{4,12},{5,13},{6,14},{7,15},{8,16},{9,17... | collective-permute-start | bytes 798728 | tf_op jit(solution)/shard_map/ppermute | solution.py:36
  62.3 1.3 %shard_map.68 = f32[264,8,128]{2,1,0:T(8,128)S(1)} custom-call(f32[65,8,128]{2,1,0:T(8,128)S(1)} %get-tuple-element.73.refs_0_, f32[65,8,128]{2,1,0:T(8,128)S(1)} %collective-permute-done.3.refs_1_, f32[65,8,128]{2,1,0:T(8,128)S(1)} %collective-permute-done.7.refs_2_, f32[65,8,128]{2,1,0:T(8,128)S(1)} %collective-permute-done.11.refs_3_), custom_call_target="tpu_custom_call" | custom-call | flops 4294967296 | bytes 1048576 | tf_op jit(solution)/shard_map/pallas_call | solution.py:332
  63.8 3.6 %collective-permute-start.19 = (f32[128,8,128]{2,1,0:T(8,128)S(1)}, f32[128,8,128]{2,1,0:T(8,128)S(1)}, u32[]{:S(2)}, u32[]{:S(2)}) collective-permute-start(f32[128,8,128]{2,1,0:T(8,128)S(1)} %get-tuple-element.89), channel_id=1, source_target_pairs={{0,1},{1,2},{2,3},{3,4},{4,5},{5,6},{6,7},{7,0},{8,9},{9,10},{10,1... | collective-permute-start | bytes 1572872 | tf_op jit(solution)/shard_map/ppermute | solution.py:40
  67.4 2.8 %collective-permute-start.23 = (f32[128,8,128]{2,1,0:T(8,128)S(1)}, f32[128,8,128]{2,1,0:T(8,128)S(1)}, u32[]{:S(2)}, u32[]{:S(2)}) collective-permute-start(f32[128,8,128]{2,1,0:T(8,128)S(1)} %get-tuple-element.90), channel_id=1, source_target_pairs={{0,7},{1,0},{2,1},{3,2},{4,3},{5,4},{6,5},{7,6},{8,15},{9,8},{10,9... | collective-permute-start | bytes 1572872 | tf_op jit(solution)/shard_map/ppermute | solution.py:40
  70.2 1.4 %collective-permute-start.9 = (f32[33,8,128]{2,1,0:T(8,128)S(1)}, f32[33,8,128]{2,1,0:T(8,128)S(1)}, u32[]{:S(2)}, u32[]{:S(2)}) collective-permute-start(f32[33,8,128]{2,1,0:T(8,128)S(1)} %get-tuple-element.61), channel_id=1, source_target_pairs={{0,16},{1,17},{2,18},{3,19},{4,20},{5,21},{6,22},{7,23},{8,24},{9,... | collective-permute-start | bytes 405512 | tf_op jit(solution)/shard_map/ppermute | solution.py:36
  71.7 1.9 %collective-permute-start.5 = (f32[33,8,128]{2,1,0:T(8,128)S(1)}, f32[33,8,128]{2,1,0:T(8,128)S(1)}, u32[]{:S(2)}, u32[]{:S(2)}) collective-permute-start(f32[33,8,128]{2,1,0:T(8,128)S(1)} %get-tuple-element.54), channel_id=1, source_target_pairs={{0,8},{1,9},{2,10},{3,11},{4,12},{5,13},{6,14},{7,15},{8,16},{9,17... | collective-permute-start | bytes 405512 | tf_op jit(solution)/shard_map/ppermute | solution.py:36
  73.5 1.3 %shard_map.67 = f32[264,8,128]{2,1,0:T(8,128)S(1)} custom-call(f32[65,8,128]{2,1,0:T(8,128)S(1)} %get-tuple-element.69.refs_0_, f32[65,8,128]{2,1,0:T(8,128)S(1)} %collective-permute-done.4.refs_1_, f32[65,8,128]{2,1,0:T(8,128)S(1)} %collective-permute-done.8.refs_2_, f32[65,8,128]{2,1,0:T(8,128)S(1)} %collective-permute-done.12.refs_3_), custom_call_target="tpu_custom_call" | custom-call | flops 4294967296 | bytes 1048576 | tf_op jit(solution)/shard_map/pallas_call | solution.py:332
  74.9 5.9 %collective-permute-done.19 = f32[128,8,128]{2,1,0:T(8,128)S(1)} collective-permute-done((f32[128,8,128]{2,1,0:T(8,128)S(1)}, f32[128,8,128]{2,1,0:T(8,128)S(1)}, u32[]{:S(2)}, u32[]{:S(2)}) %collective-permute-start.19) | collective-permute-done | bytes 524320 | tf_op jit(solution)/shard_map/ppermute | solution.py:40
  81.2 2.4 %collective-permute-start.20 = (f32[128,8,128]{2,1,0:T(8,128)S(1)}, f32[128,8,128]{2,1,0:T(8,128)S(1)}, u32[]{:S(2)}, u32[]{:S(2)}) collective-permute-start(f32[128,8,128]{2,1,0:T(8,128)S(1)} %get-tuple-element.87), channel_id=1, source_target_pairs={{0,1},{1,2},{2,3},{3,4},{4,5},{5,6},{6,7},{7,0},{8,9},{9,10},{10,1... | collective-permute-start | bytes 1572872 | tf_op jit(solution)/shard_map/ppermute | solution.py:40
  83.6 1.2 %collective-permute-start.24 = (f32[128,8,128]{2,1,0:T(8,128)S(1)}, f32[128,8,128]{2,1,0:T(8,128)S(1)}, u32[]{:S(2)}, u32[]{:S(2)}) collective-permute-start(f32[128,8,128]{2,1,0:T(8,128)S(1)} %get-tuple-element.88), channel_id=1, source_target_pairs={{0,7},{1,0},{2,1},{3,2},{4,3},{5,4},{6,5},{7,6},{8,15},{9,8},{10,9... | collective-permute-start | bytes 1572872 | tf_op jit(solution)/shard_map/ppermute | solution.py:40
  84.9 1.1 %shard_map.66 = f32[264,8,128]{2,1,0:T(8,128)S(1)} custom-call(f32[33,8,128]{2,1,0:T(8,128)S(1)} %get-tuple-element.47.refs_0_, f32[33,8,128]{2,1,0:T(8,128)S(1)} %collective-permute-done.5.refs_1_, f32[33,8,128]{2,1,0:T(8,128)S(1)} %collective-permute-done.9.refs_2_, f32[33,8,128]{2,1,0:T(8,128)S(1)} %collective-permute-done.13.refs_3_), custom_call_target="tpu_custom_call" | custom-call | flops 4294967296 | bytes 1048576 | tf_op jit(solution)/shard_map/pallas_call | solution.py:332
  85.9 6.0 %collective-permute-done.20 = f32[128,8,128]{2,1,0:T(8,128)S(1)} collective-permute-done((f32[128,8,128]{2,1,0:T(8,128)S(1)}, f32[128,8,128]{2,1,0:T(8,128)S(1)}, u32[]{:S(2)}, u32[]{:S(2)}) %collective-permute-start.20) | collective-permute-done | bytes 524320 | tf_op jit(solution)/shard_map/ppermute | solution.py:40
  92.8 1.0 %fusion.1 = f32[128,8,128]{2,1,0:T(8,128)} fusion(f32[128,8,128]{2,1,0:T(8,128)S(1)} %collective-permute-done.24, f32[128,8,128]{2,1,0:T(8,128)S(1)} %collective-permute-done.20, f32[264,8,128]{2,1,0:T(8,128)S(1)} %shard_map.66, f32[128]{0:T(128)S(1)} %convert_element_type.7), kind=kLoop, calls=%fused_computation.8 | loop fusion | flops 393216 | bytes 2097664 | tf_op jit(solution)/shard_map/mul | solution.py:374
  (41 shorter events, 4.3 us)
Async XLA Ops:
  1.1 8.1 %collective-permute-start = (f32[8,1024]{1,0:T(8,128)S(1)}, f32[8,1024]{1,0:T(8,128)S(1)}, u32[]{:S(2)}, u32[]{:S(2)}) collective-permute-start(f32[8,1024]{1,0:T(8,128)S(1)} %bitcast.10), channel_id=1, source_target_pairs={{0,1},{1,2},{2,3},{3,4},{4,5},{5,6},{6,7},{7,8},{8,9},{9,10},{10,1... | collective-permute-start | bytes 98312 | tf_op jit(solution)/shard_map/ppermute | solution.py:351
  3.1 6.1 %collective-permute-start.1 = (f32[8,1024]{1,0:T(8,128)S(1)}, f32[8,1024]{1,0:T(8,128)S(1)}, u32[]{:S(2)}, u32[]{:S(2)}) collective-permute-start(f32[8,1024]{1,0:T(8,128)S(1)} %bitcast.11), channel_id=1, source_target_pairs={{1,0},{2,1},{3,2},{4,3},{5,4},{6,5},{7,6},{8,7},{9,8},{10,9},{11,1... | collective-permute-start | bytes 98312 | tf_op jit(solution)/shard_map/ppermute | solution.py:352
  9.2 1.6 %copy-start = (f32[8,64,1024]{2,1,0:T(8,128)S(1)}, f32[8,64,1024]{2,1,0:T(8,128)}, u32[]{:S(2)}) copy-start(f32[8,64,1024]{2,1,0:T(8,128)} %param.6) | copy-start | bytes 6291460
  10.8 0.9 %copy-start.1 = (f32[64,1024]{1,0:T(8,128)S(1)}, f32[64,1024]{1,0:T(8,128)}, u32[]{:S(2)}) copy-start(f32[64,1024]{1,0:T(8,128)} %kappa.1) | copy-start | bytes 786436
  21.6 15.6 %collective-permute-start.14 = (f32[33,8,128]{2,1,0:T(8,128)S(1)}, f32[33,8,128]{2,1,0:T(8,128)S(1)}, u32[]{:S(2)}, u32[]{:S(2)}) collective-permute-start(f32[33,8,128]{2,1,0:T(8,128)S(1)} %get-tuple-element.82), channel_id=1, source_target_pairs={{0,8},{1,9},{2,10},{3,11},{4,12},{5,13},{6,14},{7,15},{8,16},{9,17... | collective-permute-start | bytes 405512 | tf_op jit(solution)/shard_map/ppermute | solution.py:36
  24.0 13.2 %collective-permute-start.15 = (f32[33,8,128]{2,1,0:T(8,128)S(1)}, f32[33,8,128]{2,1,0:T(8,128)S(1)}, u32[]{:S(2)}, u32[]{:S(2)}) collective-permute-start(f32[33,8,128]{2,1,0:T(8,128)S(1)} %get-tuple-element.83), channel_id=1, source_target_pairs={{0,16},{1,17},{2,18},{3,19},{4,20},{5,21},{6,22},{7,23},{8,24},{9,... | collective-permute-start | bytes 405512 | tf_op jit(solution)/shard_map/ppermute | solution.py:36
  24.4 12.8 %collective-permute-start.16 = (f32[33,8,128]{2,1,0:T(8,128)S(1)}, f32[33,8,128]{2,1,0:T(8,128)S(1)}, u32[]{:S(2)}, u32[]{:S(2)}) collective-permute-start(f32[33,8,128]{2,1,0:T(8,128)S(1)} %get-tuple-element.84), channel_id=1, source_target_pairs={{0,24},{1,25},{2,26},{3,27},{4,28},{5,29},{6,30},{7,31},{8,0},{9,1... | collective-permute-start | bytes 405512 | tf_op jit(solution)/shard_map/ppermute | solution.py:36
  25.0 18.5 %collective-permute-start.2 = (f32[65,8,128]{2,1,0:T(8,128)S(1)}, f32[65,8,128]{2,1,0:T(8,128)S(1)}, u32[]{:S(2)}, u32[]{:S(2)}) collective-permute-start(f32[65,8,128]{2,1,0:T(8,128)S(1)} %get-tuple-element.48), channel_id=1, source_target_pairs={{0,8},{1,9},{2,10},{3,11},{4,12},{5,13},{6,14},{7,15},{8,16},{9,17... | collective-permute-start | bytes 798728 | tf_op jit(solution)/shard_map/ppermute | solution.py:36
  27.7 15.8 %collective-permute-start.6 = (f32[65,8,128]{2,1,0:T(8,128)S(1)}, f32[65,8,128]{2,1,0:T(8,128)S(1)}, u32[]{:S(2)}, u32[]{:S(2)}) collective-permute-start(f32[65,8,128]{2,1,0:T(8,128)S(1)} %get-tuple-element.55), channel_id=1, source_target_pairs={{0,16},{1,17},{2,18},{3,19},{4,20},{5,21},{6,22},{7,23},{8,24},{9,... | collective-permute-start | bytes 798728 | tf_op jit(solution)/shard_map/ppermute | solution.py:36
  37.1 7.7 %collective-permute-start.10 = (f32[65,8,128]{2,1,0:T(8,128)S(1)}, f32[65,8,128]{2,1,0:T(8,128)S(1)}, u32[]{:S(2)}, u32[]{:S(2)}) collective-permute-start(f32[65,8,128]{2,1,0:T(8,128)S(1)} %get-tuple-element.62), channel_id=1, source_target_pairs={{0,24},{1,25},{2,26},{3,27},{4,28},{5,29},{6,30},{7,31},{8,0},{9,1... | collective-permute-start | bytes 798728 | tf_op jit(solution)/shard_map/ppermute | solution.py:36
  38.4 11.8 %collective-permute-start.17 = (f32[64,8,128]{2,1,0:T(8,128)S(1)}, f32[64,8,128]{2,1,0:T(8,128)S(1)}, u32[]{:S(2)}, u32[]{:S(2)}) collective-permute-start(f32[64,8,128]{2,1,0:T(8,128)S(1)} %get-tuple-element.93), channel_id=1, source_target_pairs={{0,1},{1,2},{2,3},{3,4},{4,5},{5,6},{6,7},{7,0},{8,9},{9,10},{10,1... | collective-permute-start | bytes 786440 | tf_op jit(solution)/shard_map/ppermute | solution.py:40
  38.5 11.7 %collective-permute-start.21 = (f32[64,8,128]{2,1,0:T(8,128)S(1)}, f32[64,8,128]{2,1,0:T(8,128)S(1)}, u32[]{:S(2)}, u32[]{:S(2)}) collective-permute-start(f32[64,8,128]{2,1,0:T(8,128)S(1)} %get-tuple-element.94), channel_id=1, source_target_pairs={{0,7},{1,0},{2,1},{3,2},{4,3},{5,4},{6,5},{7,6},{8,15},{9,8},{10,9... | collective-permute-start | bytes 786440 | tf_op jit(solution)/shard_map/ppermute | solution.py:40
  44.8 9.6 %collective-permute-start.11 = (f32[65,8,128]{2,1,0:T(8,128)S(1)}, f32[65,8,128]{2,1,0:T(8,128)S(1)}, u32[]{:S(2)}, u32[]{:S(2)}) collective-permute-start(f32[65,8,128]{2,1,0:T(8,128)S(1)} %get-tuple-element.64), channel_id=1, source_target_pairs={{0,24},{1,25},{2,26},{3,27},{4,28},{5,29},{6,30},{7,31},{8,0},{9,1... | collective-permute-start | bytes 798728 | tf_op jit(solution)/shard_map/ppermute | solution.py:36
  44.8 14.5 %collective-permute-start.7 = (f32[65,8,128]{2,1,0:T(8,128)S(1)}, f32[65,8,128]{2,1,0:T(8,128)S(1)}, u32[]{:S(2)}, u32[]{:S(2)}) collective-permute-start(f32[65,8,128]{2,1,0:T(8,128)S(1)} %get-tuple-element.57), channel_id=1, source_target_pairs={{0,16},{1,17},{2,18},{3,19},{4,20},{5,21},{6,22},{7,23},{8,24},{9,... | collective-permute-start | bytes 798728 | tf_op jit(solution)/shard_map/ppermute | solution.py:36
  46.9 13.0 %collective-permute-start.3 = (f32[65,8,128]{2,1,0:T(8,128)S(1)}, f32[65,8,128]{2,1,0:T(8,128)S(1)}, u32[]{:S(2)}, u32[]{:S(2)}) collective-permute-start(f32[65,8,128]{2,1,0:T(8,128)S(1)} %get-tuple-element.50), channel_id=1, source_target_pairs={{0,8},{1,9},{2,10},{3,11},{4,12},{5,13},{6,14},{7,15},{8,16},{9,17... | collective-permute-start | bytes 798728 | tf_op jit(solution)/shard_map/ppermute | solution.py:36
  50.3 13.3 %collective-permute-start.18 = (f32[128,8,128]{2,1,0:T(8,128)S(1)}, f32[128,8,128]{2,1,0:T(8,128)S(1)}, u32[]{:S(2)}, u32[]{:S(2)}) collective-permute-start(f32[128,8,128]{2,1,0:T(8,128)S(1)} %get-tuple-element.91), channel_id=1, source_target_pairs={{0,1},{1,2},{2,3},{3,4},{4,5},{5,6},{6,7},{7,0},{8,9},{9,10},{10,1... | collective-permute-start | bytes 1572872 | tf_op jit(solution)/shard_map/ppermute | solution.py:40
  50.5 13.1 %collective-permute-start.22 = (f32[128,8,128]{2,1,0:T(8,128)S(1)}, f32[128,8,128]{2,1,0:T(8,128)S(1)}, u32[]{:S(2)}, u32[]{:S(2)}) collective-permute-start(f32[128,8,128]{2,1,0:T(8,128)S(1)} %get-tuple-element.92), channel_id=1, source_target_pairs={{0,7},{1,0},{2,1},{3,2},{4,3},{5,4},{6,5},{7,6},{8,15},{9,8},{10,9... | collective-permute-start | bytes 1572872 | tf_op jit(solution)/shard_map/ppermute | solution.py:40
  54.5 15.7 %collective-permute-start.12 = (f32[65,8,128]{2,1,0:T(8,128)S(1)}, f32[65,8,128]{2,1,0:T(8,128)S(1)}, u32[]{:S(2)}, u32[]{:S(2)}) collective-permute-start(f32[65,8,128]{2,1,0:T(8,128)S(1)} %get-tuple-element.66), channel_id=1, source_target_pairs={{0,24},{1,25},{2,26},{3,27},{4,28},{5,29},{6,30},{7,31},{8,0},{9,1... | collective-permute-start | bytes 798728 | tf_op jit(solution)/shard_map/ppermute | solution.py:36
  59.4 10.9 %collective-permute-start.8 = (f32[65,8,128]{2,1,0:T(8,128)S(1)}, f32[65,8,128]{2,1,0:T(8,128)S(1)}, u32[]{:S(2)}, u32[]{:S(2)}) collective-permute-start(f32[65,8,128]{2,1,0:T(8,128)S(1)} %get-tuple-element.59), channel_id=1, source_target_pairs={{0,16},{1,17},{2,18},{3,19},{4,20},{5,21},{6,22},{7,23},{8,24},{9,... | collective-permute-start | bytes 798728 | tf_op jit(solution)/shard_map/ppermute | solution.py:36
  59.9 11.8 %collective-permute-start.4 = (f32[65,8,128]{2,1,0:T(8,128)S(1)}, f32[65,8,128]{2,1,0:T(8,128)S(1)}, u32[]{:S(2)}, u32[]{:S(2)}) collective-permute-start(f32[65,8,128]{2,1,0:T(8,128)S(1)} %get-tuple-element.52), channel_id=1, source_target_pairs={{0,8},{1,9},{2,10},{3,11},{4,12},{5,13},{6,14},{7,15},{8,16},{9,17... | collective-permute-start | bytes 798728 | tf_op jit(solution)/shard_map/ppermute | solution.py:36
  63.8 17.1 %collective-permute-start.19 = (f32[128,8,128]{2,1,0:T(8,128)S(1)}, f32[128,8,128]{2,1,0:T(8,128)S(1)}, u32[]{:S(2)}, u32[]{:S(2)}) collective-permute-start(f32[128,8,128]{2,1,0:T(8,128)S(1)} %get-tuple-element.89), channel_id=1, source_target_pairs={{0,1},{1,2},{2,3},{3,4},{4,5},{5,6},{6,7},{7,0},{8,9},{9,10},{10,1... | collective-permute-start | bytes 1572872 | tf_op jit(solution)/shard_map/ppermute | solution.py:40
  67.4 13.7 %collective-permute-start.23 = (f32[128,8,128]{2,1,0:T(8,128)S(1)}, f32[128,8,128]{2,1,0:T(8,128)S(1)}, u32[]{:S(2)}, u32[]{:S(2)}) collective-permute-start(f32[128,8,128]{2,1,0:T(8,128)S(1)} %get-tuple-element.90), channel_id=1, source_target_pairs={{0,7},{1,0},{2,1},{3,2},{4,3},{5,4},{6,5},{7,6},{8,15},{9,8},{10,9... | collective-permute-start | bytes 1572872 | tf_op jit(solution)/shard_map/ppermute | solution.py:40
  70.2 14.6 %collective-permute-start.13 = (f32[33,8,128]{2,1,0:T(8,128)S(1)}, f32[33,8,128]{2,1,0:T(8,128)S(1)}, u32[]{:S(2)}, u32[]{:S(2)}) collective-permute-start(f32[33,8,128]{2,1,0:T(8,128)S(1)} %get-tuple-element.68), channel_id=1, source_target_pairs={{0,24},{1,25},{2,26},{3,27},{4,28},{5,29},{6,30},{7,31},{8,0},{9,1... | collective-permute-start | bytes 405512 | tf_op jit(solution)/shard_map/ppermute | solution.py:36
  70.2 14.6 %collective-permute-start.9 = (f32[33,8,128]{2,1,0:T(8,128)S(1)}, f32[33,8,128]{2,1,0:T(8,128)S(1)}, u32[]{:S(2)}, u32[]{:S(2)}) collective-permute-start(f32[33,8,128]{2,1,0:T(8,128)S(1)} %get-tuple-element.61), channel_id=1, source_target_pairs={{0,16},{1,17},{2,18},{3,19},{4,20},{5,21},{6,22},{7,23},{8,24},{9,... | collective-permute-start | bytes 405512 | tf_op jit(solution)/shard_map/ppermute | solution.py:36
  71.7 13.2 %collective-permute-start.5 = (f32[33,8,128]{2,1,0:T(8,128)S(1)}, f32[33,8,128]{2,1,0:T(8,128)S(1)}, u32[]{:S(2)}, u32[]{:S(2)}) collective-permute-start(f32[33,8,128]{2,1,0:T(8,128)S(1)} %get-tuple-element.54), channel_id=1, source_target_pairs={{0,8},{1,9},{2,10},{3,11},{4,12},{5,13},{6,14},{7,15},{8,16},{9,17... | collective-permute-start | bytes 405512 | tf_op jit(solution)/shard_map/ppermute | solution.py:36
  74.9 10.0 %copy-start.2 = (s32[128]{0:T(128)S(1)}, s32[128]{0:T(128)}, u32[]{:S(2)}) copy-start(s32[128]{0:T(128)} %param.11) | copy-start | bytes 1540
  81.2 10.7 %collective-permute-start.20 = (f32[128,8,128]{2,1,0:T(8,128)S(1)}, f32[128,8,128]{2,1,0:T(8,128)S(1)}, u32[]{:S(2)}, u32[]{:S(2)}) collective-permute-start(f32[128,8,128]{2,1,0:T(8,128)S(1)} %get-tuple-element.87), channel_id=1, source_target_pairs={{0,1},{1,2},{2,3},{3,4},{4,5},{5,6},{6,7},{7,0},{8,9},{9,10},{10,1... | collective-permute-start | bytes 1572872 | tf_op jit(solution)/shard_map/ppermute | solution.py:40
  83.6 9.2 %collective-permute-start.24 = (f32[128,8,128]{2,1,0:T(8,128)S(1)}, f32[128,8,128]{2,1,0:T(8,128)S(1)}, u32[]{:S(2)}, u32[]{:S(2)}) collective-permute-start(f32[128,8,128]{2,1,0:T(8,128)S(1)} %get-tuple-element.88), channel_id=1, source_target_pairs={{0,7},{1,0},{2,1},{3,2},{4,3},{5,4},{6,5},{7,6},{8,15},{9,8},{10,9... | collective-permute-start | bytes 1572872 | tf_op jit(solution)/shard_map/ppermute | solution.py:40

commit v3 on v2

--- a/solution.py
+++ b/solution.py
@@ -15,7 +15,7 @@
 GROUP = 16
 PART = 32
 WEIGHT_PARTS = PAIRS // PART
-FAR_VMEM, NEAR_VMEM = 44, 44
+FAR_VMEM, NEAR_VMEM = 50, 44
 DISTANCES = (4, 3, 2, 1, 0)
 SIZES = (CAP, 2 * CAP, 2 * CAP, 2 * CAP, CAP)
 STARTS = tuple(X * (sum(SIZES[:n]) + n) for n in range(len(SIZES) + 1))
@@ -181,7 +181,7 @@
             rows[r * per + c] = value[:, c * B : (c + 1) * B]
         return cur, nxt
 
-    lax.fori_loop(0, ROWS, step, (above, row(0)), unroll=2)
+    lax.fori_loop(0, ROWS, step, (above, row(0)), unroll=4)
     save = pltpu.make_async_copy(rows, smooth, sem.at[0])
     save.start()
     put_targets(lambda k: table[k : k + 1], send, 0, FAR, 0)

time: 94.1 us -> 93.8 us (level)
  waiting for transfers between devices: 20.6 us -> 23.3 us
  starting transfers between devices: 43.8 us -> 41.3 us
  local copies, waits for them, and re-layouts: 3.68 us -> 2.09 us
  Pallas kernels: 23.5 us -> 24.8 us
    ppermute x15, starting transfers between devices: 18.1 us -> 16.1 us  [send_x(): return lax.ppermute(a, 'tile', shift(dx, 0))]
    unnamed x8 -> x6, local copies, waits for them, and re-layouts: 2.56 us -> 0.97 us
    ppermute x8, waiting for transfers between devices: 13.1 us -> 14.6 us  [send_z(): return lax.ppermute(a, 'tile', shift(0, dz))]
    ppermute x15, waiting for transfers between devices: 6.44 us -> 7.57 us  [send_x(): return lax.ppermute(a, 'tile', shift(dx, 0))]
    pallas_call x1, Pallas kernels: 9.81 us -> 10.9 us  [remap_far(): pl.pallas_call(far_kernel, out_shape=[jax.ShapeDtypeStruct((ROWS * COLS /...]
  transfers between devices with their start and end apart: 25 -> 25, of which waited for: 8 -> 10; matrix products, arithmetic and copies ran while one was open for 1% -> 1% of each run, Pallas kernels for 15% -> 15%
where the time goes in v3:
time: 93.8 us
  starting transfers between devices  41.3 us (44%)
  Pallas kernels  24.8 us (26%)
  waiting for transfers between devices  23.3 us (25%)
  local copies, waits for them, and re-layouts  2.09 us (2%)
  other arithmetic  2.07 us (2%)
    ppermute x8, starting transfers between devices, send_z(): return lax.ppermute(a, 'tile', shift(0, dz))  18.9 us
    ppermute x15, starting transfers between devices, send_x(): return lax.ppermute(a, 'tile', shift(dx, 0))  16.1 us
    ppermute x8, waiting for transfers between devices, send_z(): return lax.ppermute(a, 'tile', shift(0, dz))  14.6 us
    pallas_call x1, Pallas kernels, remap_far(): pl.pallas_call(far_kernel, out_shape=[jax.ShapeDtypeStruct((ROWS * COLS /...  10.9 us
    ppermute x15, waiting for transfers between devices, send_x(): return lax.ppermute(a, 'tile', shift(dx, 0))  7.57 us
    pallas_call x1, Pallas kernels, remap_near(): pl.pallas_call(near_kernel, out_shape=shapes, in_specs=[pl.BlockSpec(memo...  7.52 us
    pallas_call x5, Pallas kernels, gather_class(): pl.pallas_call(lambda *refs: gather_kernel(size, *refs), out_shape=jax.Sh...  6.33 us
    ppermute x1, starting transfers between devices, body(): lax.ppermute(atmos[:, 0, :], 'tile', [((i + 1) % tiles, i) for i in range...  4.3 us
  transfers between devices with their start and end apart: 25, of which 10 were waited for; matrix products, arithmetic and copies ran while one was open for 1% of the time, Pallas kernels for 15%

profile of v3, /device:TPU:6, one launch (start us, length us, event | category | flops | bytes accessed | tf_op | source)
XLA Modules:
  0.0 93.8 jit_solution(2771978085010267478)
XLA Ops:
  0.0 1.1 %fusion.2 = (f32[8,1,1024]{2,1,0:T(1,128)S(1)}, f32[8,1,1024]{2,1,0:T(1,128)S(1)}) fusion(f32[8,64,1024]{2,1,0:T(8,128)} %param.6), kind=kLoop, calls=%fused_computation.12 | loop fusion | bytes 131072 | tf_op jit(solution)/shard_map/slice | solution.py:352
  1.1 2.0 %collective-permute-start = (f32[8,1024]{1,0:T(8,128)S(1)}, f32[8,1024]{1,0:T(8,128)S(1)}, u32[]{:S(2)}, u32[]{:S(2)}) collective-permute-start(f32[8,1024]{1,0:T(8,128)S(1)} %bitcast.10), channel_id=1, source_target_pairs={{0,1},{1,2},{2,3},{3,4},{4,5},{5,6},{6,7},{7,8},{8,9},{9,10},{10,1... | collective-permute-start | bytes 98312 | tf_op jit(solution)/shard_map/ppermute | solution.py:351
  3.1 4.3 %collective-permute-start.1 = (f32[8,1024]{1,0:T(8,128)S(1)}, f32[8,1024]{1,0:T(8,128)S(1)}, u32[]{:S(2)}, u32[]{:S(2)}) collective-permute-start(f32[8,1024]{1,0:T(8,128)S(1)} %bitcast.11), channel_id=1, source_target_pairs={{1,0},{2,1},{3,2},{4,3},{5,4},{6,5},{7,6},{8,7},{9,8},{10,9},{11,1... | collective-permute-start | bytes 98312 | tf_op jit(solution)/shard_map/ppermute | solution.py:352
  8.1 1.1 %collective-permute-done.north = f32[8,1024]{1,0:T(8,128)S(1)} collective-permute-done((f32[8,1024]{1,0:T(8,128)S(1)}, f32[8,1024]{1,0:T(8,128)S(1)}, u32[]{:S(2)}, u32[]{:S(2)}) %collective-permute-start) | collective-permute-done | bytes 32800 | tf_op jit(solution)/shard_map/ppermute | solution.py:351
  9.2 0.9 %copy-done = f32[64,1024]{1,0:T(8,128)S(1)} copy-done((f32[64,1024]{1,0:T(8,128)S(1)}, f32[64,1024]{1,0:T(8,128)}, u32[]{:S(2)}) %copy-start) | copy-done | bytes 262168
  10.1 10.9 %shard_map.64 = (f32[512,8,128]{2,1,0:T(8,128)S(1)}, s32[6,512]{1,0:T(8,128)S(1)}, f32[33,8,128]{2,1,0:T(8,128)S(1)}, f32[33,8,128]{2,1,0:T(8,128)S(1)}, f32[33,...) custom-call(f32[512,1024]{1,0:T(8,128)} %bitcast.9, ...), custom_call_target="tpu_custom_call" | custom-call | flops 1048576 | bytes 20971520 | tf_op jit(solution)/shard_map/pallas_call | solution.py:258
  21.1 2.5 %collective-permute-start.14 = (f32[33,8,128]{2,1,0:T(8,128)S(1)}, f32[33,8,128]{2,1,0:T(8,128)S(1)}, u32[]{:S(2)}, u32[]{:S(2)}) collective-permute-start(f32[33,8,128]{2,1,0:T(8,128)S(1)} %get-tuple-element.82), channel_id=1, source_target_pairs={{0,8},{1,9},{2,10},{3,11},{4,12},{5,13},{6,14},{7,15},{8,16},{9,17... | collective-permute-start | bytes 405512 | tf_op jit(solution)/shard_map/ppermute | solution.py:36
  23.6 1.0 %collective-permute-start.16 = (f32[33,8,128]{2,1,0:T(8,128)S(1)}, f32[33,8,128]{2,1,0:T(8,128)S(1)}, u32[]{:S(2)}, u32[]{:S(2)}) collective-permute-start(f32[33,8,128]{2,1,0:T(8,128)S(1)} %get-tuple-element.84), channel_id=1, source_target_pairs={{0,24},{1,25},{2,26},{3,27},{4,28},{5,29},{6,30},{7,31},{8,0},{9,1... | collective-permute-start | bytes 405512 | tf_op jit(solution)/shard_map/ppermute | solution.py:36
  24.5 2.3 %collective-permute-start.2 = (f32[65,8,128]{2,1,0:T(8,128)S(1)}, f32[65,8,128]{2,1,0:T(8,128)S(1)}, u32[]{:S(2)}, u32[]{:S(2)}) collective-permute-start(f32[65,8,128]{2,1,0:T(8,128)S(1)} %get-tuple-element.48), channel_id=1, source_target_pairs={{0,8},{1,9},{2,10},{3,11},{4,12},{5,13},{6,14},{7,15},{8,16},{9,17... | collective-permute-start | bytes 798728 | tf_op jit(solution)/shard_map/ppermute | solution.py:36
  26.8 2.3 %collective-permute-start.6 = (f32[65,8,128]{2,1,0:T(8,128)S(1)}, f32[65,8,128]{2,1,0:T(8,128)S(1)}, u32[]{:S(2)}, u32[]{:S(2)}) collective-permute-start(f32[65,8,128]{2,1,0:T(8,128)S(1)} %get-tuple-element.55), channel_id=1, source_target_pairs={{0,16},{1,17},{2,18},{3,19},{4,20},{5,21},{6,22},{7,23},{8,24},{9,... | collective-permute-start | bytes 798728 | tf_op jit(solution)/shard_map/ppermute | solution.py:36
  29.1 7.5 %shard_map.65 = (f32[65,8,128]{2,1,0:T(8,128)S(1)}, f32[65,8,128]{2,1,0:T(8,128)S(1)}, f32[65,8,128]{2,1,0:T(8,128)S(1)}, f32[65,8,128]{2,1,0:T(8,128)S(1)}, f32...) custom-call(s32[6,512]{1,0:T(8,128)S(1)} %get-tuple-element.45.meta,, ...), custom_call_target="tpu_custom_call" | custom-call | flops 8589934592 | bytes 25165824 | tf_op jit(solution)/shard_map/pallas_call | solution.py:291
  36.8 1.0 %shard_map.70 = f32[264,8,128]{2,1,0:T(8,128)S(1)} custom-call(f32[33,8,128]{2,1,0:T(8,128)S(1)} %get-tuple-element.81.refs_0_, f32[33,8,128]{2,1,0:T(8,128)S(1)} %collective-permute-done.14.refs_1_, f32[33,8,128]{2,1,0:T(8,128)S(1)} %collective-permute-done.15.refs_2_, f32[33,8,128]{2,1,0:T(8,128)S(1)} %collective-permute-done.16.refs_3_), custom_call_target="tpu_custom_call" | custom-call | flops 4294967296 | bytes 1048576 | tf_op jit(solution)/shard_map/pallas_call | solution.py:332
  37.9 4.7 %collective-permute-start.21 = (f32[64,8,128]{2,1,0:T(8,128)S(1)}, f32[64,8,128]{2,1,0:T(8,128)S(1)}, u32[]{:S(2)}, u32[]{:S(2)}) collective-permute-start(f32[64,8,128]{2,1,0:T(8,128)S(1)} %get-tuple-element.94), channel_id=1, source_target_pairs={{0,7},{1,0},{2,1},{3,2},{4,3},{5,4},{6,5},{7,6},{8,15},{9,8},{10,9... | collective-permute-start | bytes 786440 | tf_op jit(solution)/shard_map/ppermute | solution.py:40
  42.7 1.7 %collective-permute-done.10.refs_3_ = f32[65,8,128]{2,1,0:T(8,128)S(1)} collective-permute-done((f32[65,8,128]{2,1,0:T(8,128)S(1)}, f32[65,8,128]{2,1,0:T(8,128)S(1)}, u32[]{:S(2)}, u32[]{:S(2)}) %collective-permute-start.10) | collective-permute-done | bytes 266272 | tf_op jit(solution)/shard_map/ppermute | solution.py:36
  44.4 1.7 %collective-permute-start.7 = (f32[65,8,128]{2,1,0:T(8,128)S(1)}, f32[65,8,128]{2,1,0:T(8,128)S(1)}, u32[]{:S(2)}, u32[]{:S(2)}) collective-permute-start(f32[65,8,128]{2,1,0:T(8,128)S(1)} %get-tuple-element.57), channel_id=1, source_target_pairs={{0,16},{1,17},{2,18},{3,19},{4,20},{5,21},{6,22},{7,23},{8,24},{9,... | collective-permute-start | bytes 798728 | tf_op jit(solution)/shard_map/ppermute | solution.py:36
  46.0 1.6 %collective-permute-start.3 = (f32[65,8,128]{2,1,0:T(8,128)S(1)}, f32[65,8,128]{2,1,0:T(8,128)S(1)}, u32[]{:S(2)}, u32[]{:S(2)}) collective-permute-start(f32[65,8,128]{2,1,0:T(8,128)S(1)} %get-tuple-element.50), channel_id=1, source_target_pairs={{0,8},{1,9},{2,10},{3,11},{4,12},{5,13},{6,14},{7,15},{8,16},{9,17... | collective-permute-start | bytes 798728 | tf_op jit(solution)/shard_map/ppermute | solution.py:36
  47.7 1.5 %shard_map.69 = f32[264,8,128]{2,1,0:T(8,128)S(1)} custom-call(f32[65,8,128]{2,1,0:T(8,128)S(1)} %get-tuple-element.77.refs_0_, f32[65,8,128]{2,1,0:T(8,128)S(1)} %collective-permute-done.2.refs_1_, f32[65,8,128]{2,1,0:T(8,128)S(1)} %collective-permute-done.6.refs_2_, f32[65,8,128]{2,1,0:T(8,128)S(1)} %collective-permute-done.10.refs_3_), custom_call_target="tpu_custom_call" | custom-call | flops 4294967296 | bytes 1048576 | tf_op jit(solution)/shard_map/pallas_call | solution.py:332
  49.3 0.9 collective-permute-start.18
  50.2 4.2 %collective-permute-start.22 = (f32[128,8,128]{2,1,0:T(8,128)S(1)}, f32[128,8,128]{2,1,0:T(8,128)S(1)}, u32[]{:S(2)}, u32[]{:S(2)}) collective-permute-start(f32[128,8,128]{2,1,0:T(8,128)S(1)} %get-tuple-element.92), channel_id=1, source_target_pairs={{0,7},{1,0},{2,1},{3,2},{4,3},{5,4},{6,5},{7,6},{8,15},{9,8},{10,9... | collective-permute-start | bytes 1572872 | tf_op jit(solution)/shard_map/ppermute | solution.py:40
  54.4 4.3 %collective-permute-done.7.refs_2_ = f32[65,8,128]{2,1,0:T(8,128)S(1)} collective-permute-done((f32[65,8,128]{2,1,0:T(8,128)S(1)}, f32[65,8,128]{2,1,0:T(8,128)S(1)}, u32[]{:S(2)}, u32[]{:S(2)}) %collective-permute-start.7) | collective-permute-done | bytes 266272 | tf_op jit(solution)/shard_map/ppermute | solution.py:36
  59.2 1.9 %collective-permute-start.4 = (f32[65,8,128]{2,1,0:T(8,128)S(1)}, f32[65,8,128]{2,1,0:T(8,128)S(1)}, u32[]{:S(2)}, u32[]{:S(2)}) collective-permute-start(f32[65,8,128]{2,1,0:T(8,128)S(1)} %get-tuple-element.52), channel_id=1, source_target_pairs={{0,8},{1,9},{2,10},{3,11},{4,12},{5,13},{6,14},{7,15},{8,16},{9,17... | collective-permute-start | bytes 798728 | tf_op jit(solution)/shard_map/ppermute | solution.py:36
  61.2 1.3 %shard_map.68 = f32[264,8,128]{2,1,0:T(8,128)S(1)} custom-call(f32[65,8,128]{2,1,0:T(8,128)S(1)} %get-tuple-element.73.refs_0_, f32[65,8,128]{2,1,0:T(8,128)S(1)} %collective-permute-done.3.refs_1_, f32[65,8,128]{2,1,0:T(8,128)S(1)} %collective-permute-done.7.refs_2_, f32[65,8,128]{2,1,0:T(8,128)S(1)} %collective-permute-done.11.refs_3_), custom_call_target="tpu_custom_call" | custom-call | flops 4294967296 | bytes 1048576 | tf_op jit(solution)/shard_map/pallas_call | solution.py:332
  62.6 4.7 %collective-permute-start.19 = (f32[128,8,128]{2,1,0:T(8,128)S(1)}, f32[128,8,128]{2,1,0:T(8,128)S(1)}, u32[]{:S(2)}, u32[]{:S(2)}) collective-permute-start(f32[128,8,128]{2,1,0:T(8,128)S(1)} %get-tuple-element.89), channel_id=1, source_target_pairs={{0,1},{1,2},{2,3},{3,4},{4,5},{5,6},{6,7},{7,0},{8,9},{9,10},{10,1... | collective-permute-start | bytes 1572872 | tf_op jit(solution)/shard_map/ppermute | solution.py:40
  70.3 1.8 %collective-permute-start.5 = (f32[33,8,128]{2,1,0:T(8,128)S(1)}, f32[33,8,128]{2,1,0:T(8,128)S(1)}, u32[]{:S(2)}, u32[]{:S(2)}) collective-permute-start(f32[33,8,128]{2,1,0:T(8,128)S(1)} %get-tuple-element.54), channel_id=1, source_target_pairs={{0,8},{1,9},{2,10},{3,11},{4,12},{5,13},{6,14},{7,15},{8,16},{9,17... | collective-permute-start | bytes 405512 | tf_op jit(solution)/shard_map/ppermute | solution.py:36
  72.1 1.3 %shard_map.67 = f32[264,8,128]{2,1,0:T(8,128)S(1)} custom-call(f32[65,8,128]{2,1,0:T(8,128)S(1)} %get-tuple-element.69.refs_0_, f32[65,8,128]{2,1,0:T(8,128)S(1)} %collective-permute-done.4.refs_1_, f32[65,8,128]{2,1,0:T(8,128)S(1)} %collective-permute-done.8.refs_2_, f32[65,8,128]{2,1,0:T(8,128)S(1)} %collective-permute-done.12.refs_3_), custom_call_target="tpu_custom_call" | custom-call | flops 4294967296 | bytes 1048576 | tf_op jit(solution)/shard_map/pallas_call | solution.py:332
  73.4 4.3 %collective-permute-done.19 = f32[128,8,128]{2,1,0:T(8,128)S(1)} collective-permute-done((f32[128,8,128]{2,1,0:T(8,128)S(1)}, f32[128,8,128]{2,1,0:T(8,128)S(1)}, u32[]{:S(2)}, u32[]{:S(2)}) %collective-permute-start.19) | collective-permute-done | bytes 524320 | tf_op jit(solution)/shard_map/ppermute | solution.py:40
  77.6 3.4 %collective-permute-done.23 = f32[128,8,128]{2,1,0:T(8,128)S(1)} collective-permute-done((f32[128,8,128]{2,1,0:T(8,128)S(1)}, f32[128,8,128]{2,1,0:T(8,128)S(1)}, u32[]{:S(2)}, u32[]{:S(2)}) %collective-permute-start.23) | collective-permute-done | bytes 524320 | tf_op jit(solution)/shard_map/ppermute | solution.py:40
  81.1 2.4 %collective-permute-start.20 = (f32[128,8,128]{2,1,0:T(8,128)S(1)}, f32[128,8,128]{2,1,0:T(8,128)S(1)}, u32[]{:S(2)}, u32[]{:S(2)}) collective-permute-start(f32[128,8,128]{2,1,0:T(8,128)S(1)} %get-tuple-element.87), channel_id=1, source_target_pairs={{0,1},{1,2},{2,3},{3,4},{4,5},{5,6},{6,7},{7,0},{8,9},{9,10},{10,1... | collective-permute-start | bytes 1572872 | tf_op jit(solution)/shard_map/ppermute | solution.py:40
  84.5 1.3 %shard_map.66 = f32[264,8,128]{2,1,0:T(8,128)S(1)} custom-call(f32[33,8,128]{2,1,0:T(8,128)S(1)} %get-tuple-element.47.refs_0_, f32[33,8,128]{2,1,0:T(8,128)S(1)} %collective-permute-done.5.refs_1_, f32[33,8,128]{2,1,0:T(8,128)S(1)} %collective-permute-done.9.refs_2_, f32[33,8,128]{2,1,0:T(8,128)S(1)} %collective-permute-done.13.refs_3_), custom_call_target="tpu_custom_call" | custom-call | flops 4294967296 | bytes 1048576 | tf_op jit(solution)/shard_map/pallas_call | solution.py:332
  85.8 5.8 %collective-permute-done.20 = f32[128,8,128]{2,1,0:T(8,128)S(1)} collective-permute-done((f32[128,8,128]{2,1,0:T(8,128)S(1)}, f32[128,8,128]{2,1,0:T(8,128)S(1)}, u32[]{:S(2)}, u32[]{:S(2)}) %collective-permute-start.20) | collective-permute-done | bytes 524320 | tf_op jit(solution)/shard_map/ppermute | solution.py:40
  91.6 1.1 %collective-permute-done.24 = f32[128,8,128]{2,1,0:T(8,128)S(1)} collective-permute-done((f32[128,8,128]{2,1,0:T(8,128)S(1)}, f32[128,8,128]{2,1,0:T(8,128)S(1)}, u32[]{:S(2)}, u32[]{:S(2)}) %collective-permute-start.24) | collective-permute-done | bytes 524320 | tf_op jit(solution)/shard_map/ppermute | solution.py:40
  92.7 1.0 %fusion.1 = f32[128,8,128]{2,1,0:T(8,128)} fusion(f32[128,8,128]{2,1,0:T(8,128)S(1)} %collective-permute-done.24, f32[128,8,128]{2,1,0:T(8,128)S(1)} %collective-permute-done.20, f32[264,8,128]{2,1,0:T(8,128)S(1)} %shard_map.66, f32[128]{0:T(128)S(1)} %convert_element_type.7), kind=kLoop, calls=%fused_computation.8 | loop fusion | flops 393216 | bytes 2097664 | tf_op jit(solution)/shard_map/mul | solution.py:374
  (39 shorter events, 5.7 us)
Async XLA Ops:
  1.1 8.1 %collective-permute-start = (f32[8,1024]{1,0:T(8,128)S(1)}, f32[8,1024]{1,0:T(8,128)S(1)}, u32[]{:S(2)}, u32[]{:S(2)}) collective-permute-start(f32[8,1024]{1,0:T(8,128)S(1)} %bitcast.10), channel_id=1, source_target_pairs={{0,1},{1,2},{2,3},{3,4},{4,5},{5,6},{6,7},{7,8},{8,9},{9,10},{10,1... | collective-permute-start | bytes 98312 | tf_op jit(solution)/shard_map/ppermute | solution.py:351
  3.1 6.1 %collective-permute-start.1 = (f32[8,1024]{1,0:T(8,128)S(1)}, f32[8,1024]{1,0:T(8,128)S(1)}, u32[]{:S(2)}, u32[]{:S(2)}) collective-permute-start(f32[8,1024]{1,0:T(8,128)S(1)} %bitcast.11), channel_id=1, source_target_pairs={{1,0},{2,1},{3,2},{4,3},{5,4},{6,5},{7,6},{8,7},{9,8},{10,9},{11,1... | collective-permute-start | bytes 98312 | tf_op jit(solution)/shard_map/ppermute | solution.py:352
  9.2 1.0 %copy-start = (f32[64,1024]{1,0:T(8,128)S(1)}, f32[64,1024]{1,0:T(8,128)}, u32[]{:S(2)}) copy-start(f32[64,1024]{1,0:T(8,128)} %kappa.1) | copy-start | bytes 786436
  21.1 15.6 %collective-permute-start.14 = (f32[33,8,128]{2,1,0:T(8,128)S(1)}, f32[33,8,128]{2,1,0:T(8,128)S(1)}, u32[]{:S(2)}, u32[]{:S(2)}) collective-permute-start(f32[33,8,128]{2,1,0:T(8,128)S(1)} %get-tuple-element.82), channel_id=1, source_target_pairs={{0,8},{1,9},{2,10},{3,11},{4,12},{5,13},{6,14},{7,15},{8,16},{9,17... | collective-permute-start | bytes 405512 | tf_op jit(solution)/shard_map/ppermute | solution.py:36
  23.6 13.2 %collective-permute-start.15 = (f32[33,8,128]{2,1,0:T(8,128)S(1)}, f32[33,8,128]{2,1,0:T(8,128)S(1)}, u32[]{:S(2)}, u32[]{:S(2)}) collective-permute-start(f32[33,8,128]{2,1,0:T(8,128)S(1)} %get-tuple-element.83), channel_id=1, source_target_pairs={{0,16},{1,17},{2,18},{3,19},{4,20},{5,21},{6,22},{7,23},{8,24},{9,... | collective-permute-start | bytes 405512 | tf_op jit(solution)/shard_map/ppermute | solution.py:36
  23.6 13.2 %collective-permute-start.16 = (f32[33,8,128]{2,1,0:T(8,128)S(1)}, f32[33,8,128]{2,1,0:T(8,128)S(1)}, u32[]{:S(2)}, u32[]{:S(2)}) collective-permute-start(f32[33,8,128]{2,1,0:T(8,128)S(1)} %get-tuple-element.84), channel_id=1, source_target_pairs={{0,24},{1,25},{2,26},{3,27},{4,28},{5,29},{6,30},{7,31},{8,0},{9,1... | collective-permute-start | bytes 405512 | tf_op jit(solution)/shard_map/ppermute | solution.py:36
  24.5 18.1 %collective-permute-start.2 = (f32[65,8,128]{2,1,0:T(8,128)S(1)}, f32[65,8,128]{2,1,0:T(8,128)S(1)}, u32[]{:S(2)}, u32[]{:S(2)}) collective-permute-start(f32[65,8,128]{2,1,0:T(8,128)S(1)} %get-tuple-element.48), channel_id=1, source_target_pairs={{0,8},{1,9},{2,10},{3,11},{4,12},{5,13},{6,14},{7,15},{8,16},{9,17... | collective-permute-start | bytes 798728 | tf_op jit(solution)/shard_map/ppermute | solution.py:36
  26.8 15.9 %collective-permute-start.6 = (f32[65,8,128]{2,1,0:T(8,128)S(1)}, f32[65,8,128]{2,1,0:T(8,128)S(1)}, u32[]{:S(2)}, u32[]{:S(2)}) collective-permute-start(f32[65,8,128]{2,1,0:T(8,128)S(1)} %get-tuple-element.55), channel_id=1, source_target_pairs={{0,16},{1,17},{2,18},{3,19},{4,20},{5,21},{6,22},{7,23},{8,24},{9,... | collective-permute-start | bytes 798728 | tf_op jit(solution)/shard_map/ppermute | solution.py:36
  36.7 7.7 %collective-permute-start.10 = (f32[65,8,128]{2,1,0:T(8,128)S(1)}, f32[65,8,128]{2,1,0:T(8,128)S(1)}, u32[]{:S(2)}, u32[]{:S(2)}) collective-permute-start(f32[65,8,128]{2,1,0:T(8,128)S(1)} %get-tuple-element.62), channel_id=1, source_target_pairs={{0,24},{1,25},{2,26},{3,27},{4,28},{5,29},{6,30},{7,31},{8,0},{9,1... | collective-permute-start | bytes 798728 | tf_op jit(solution)/shard_map/ppermute | solution.py:36
  37.8 11.3 %collective-permute-start.17 = (f32[64,8,128]{2,1,0:T(8,128)S(1)}, f32[64,8,128]{2,1,0:T(8,128)S(1)}, u32[]{:S(2)}, u32[]{:S(2)}) collective-permute-start(f32[64,8,128]{2,1,0:T(8,128)S(1)} %get-tuple-element.93), channel_id=1, source_target_pairs={{0,1},{1,2},{2,3},{3,4},{4,5},{5,6},{6,7},{7,0},{8,9},{9,10},{10,1... | collective-permute-start | bytes 786440 | tf_op jit(solution)/shard_map/ppermute | solution.py:40
  37.9 11.2 %collective-permute-start.21 = (f32[64,8,128]{2,1,0:T(8,128)S(1)}, f32[64,8,128]{2,1,0:T(8,128)S(1)}, u32[]{:S(2)}, u32[]{:S(2)}) collective-permute-start(f32[64,8,128]{2,1,0:T(8,128)S(1)} %get-tuple-element.94), channel_id=1, source_target_pairs={{0,7},{1,0},{2,1},{3,2},{4,3},{5,4},{6,5},{7,6},{8,15},{9,8},{10,9... | collective-permute-start | bytes 786440 | tf_op jit(solution)/shard_map/ppermute | solution.py:40
  44.4 10.1 %collective-permute-start.11 = (f32[65,8,128]{2,1,0:T(8,128)S(1)}, f32[65,8,128]{2,1,0:T(8,128)S(1)}, u32[]{:S(2)}, u32[]{:S(2)}) collective-permute-start(f32[65,8,128]{2,1,0:T(8,128)S(1)} %get-tuple-element.64), channel_id=1, source_target_pairs={{0,24},{1,25},{2,26},{3,27},{4,28},{5,29},{6,30},{7,31},{8,0},{9,1... | collective-permute-start | bytes 798728 | tf_op jit(solution)/shard_map/ppermute | solution.py:36
  44.4 14.3 %collective-permute-start.7 = (f32[65,8,128]{2,1,0:T(8,128)S(1)}, f32[65,8,128]{2,1,0:T(8,128)S(1)}, u32[]{:S(2)}, u32[]{:S(2)}) collective-permute-start(f32[65,8,128]{2,1,0:T(8,128)S(1)} %get-tuple-element.57), channel_id=1, source_target_pairs={{0,16},{1,17},{2,18},{3,19},{4,20},{5,21},{6,22},{7,23},{8,24},{9,... | collective-permute-start | bytes 798728 | tf_op jit(solution)/shard_map/ppermute | solution.py:36
  46.0 13.2 %collective-permute-start.3 = (f32[65,8,128]{2,1,0:T(8,128)S(1)}, f32[65,8,128]{2,1,0:T(8,128)S(1)}, u32[]{:S(2)}, u32[]{:S(2)}) collective-permute-start(f32[65,8,128]{2,1,0:T(8,128)S(1)} %get-tuple-element.50), channel_id=1, source_target_pairs={{0,8},{1,9},{2,10},{3,11},{4,12},{5,13},{6,14},{7,15},{8,16},{9,17... | collective-permute-start | bytes 798728 | tf_op jit(solution)/shard_map/ppermute | solution.py:36
  49.3 13.1 %collective-permute-start.18 = (f32[128,8,128]{2,1,0:T(8,128)S(1)}, f32[128,8,128]{2,1,0:T(8,128)S(1)}, u32[]{:S(2)}, u32[]{:S(2)}) collective-permute-start(f32[128,8,128]{2,1,0:T(8,128)S(1)} %get-tuple-element.91), channel_id=1, source_target_pairs={{0,1},{1,2},{2,3},{3,4},{4,5},{5,6},{6,7},{7,0},{8,9},{9,10},{10,1... | collective-permute-start | bytes 1572872 | tf_op jit(solution)/shard_map/ppermute | solution.py:40
  50.2 12.2 %collective-permute-start.22 = (f32[128,8,128]{2,1,0:T(8,128)S(1)}, f32[128,8,128]{2,1,0:T(8,128)S(1)}, u32[]{:S(2)}, u32[]{:S(2)}) collective-permute-start(f32[128,8,128]{2,1,0:T(8,128)S(1)} %get-tuple-element.92), channel_id=1, source_target_pairs={{0,7},{1,0},{2,1},{3,2},{4,3},{5,4},{6,5},{7,6},{8,15},{9,8},{10,9... | collective-permute-start | bytes 1572872 | tf_op jit(solution)/shard_map/ppermute | solution.py:40
  54.4 13.8 %collective-permute-start.12 = (f32[65,8,128]{2,1,0:T(8,128)S(1)}, f32[65,8,128]{2,1,0:T(8,128)S(1)}, u32[]{:S(2)}, u32[]{:S(2)}) collective-permute-start(f32[65,8,128]{2,1,0:T(8,128)S(1)} %get-tuple-element.66), channel_id=1, source_target_pairs={{0,24},{1,25},{2,26},{3,27},{4,28},{5,29},{6,30},{7,31},{8,0},{9,1... | collective-permute-start | bytes 798728 | tf_op jit(solution)/shard_map/ppermute | solution.py:36
  58.7 10.3 %collective-permute-start.8 = (f32[65,8,128]{2,1,0:T(8,128)S(1)}, f32[65,8,128]{2,1,0:T(8,128)S(1)}, u32[]{:S(2)}, u32[]{:S(2)}) collective-permute-start(f32[65,8,128]{2,1,0:T(8,128)S(1)} %get-tuple-element.59), channel_id=1, source_target_pairs={{0,16},{1,17},{2,18},{3,19},{4,20},{5,21},{6,22},{7,23},{8,24},{9,... | collective-permute-start | bytes 798728 | tf_op jit(solution)/shard_map/ppermute | solution.py:36
  59.2 11.0 %collective-permute-start.4 = (f32[65,8,128]{2,1,0:T(8,128)S(1)}, f32[65,8,128]{2,1,0:T(8,128)S(1)}, u32[]{:S(2)}, u32[]{:S(2)}) collective-permute-start(f32[65,8,128]{2,1,0:T(8,128)S(1)} %get-tuple-element.52), channel_id=1, source_target_pairs={{0,8},{1,9},{2,10},{3,11},{4,12},{5,13},{6,14},{7,15},{8,16},{9,17... | collective-permute-start | bytes 798728 | tf_op jit(solution)/shard_map/ppermute | solution.py:36
  62.6 15.1 %collective-permute-start.19 = (f32[128,8,128]{2,1,0:T(8,128)S(1)}, f32[128,8,128]{2,1,0:T(8,128)S(1)}, u32[]{:S(2)}, u32[]{:S(2)}) collective-permute-start(f32[128,8,128]{2,1,0:T(8,128)S(1)} %get-tuple-element.89), channel_id=1, source_target_pairs={{0,1},{1,2},{2,3},{3,4},{4,5},{5,6},{6,7},{7,0},{8,9},{9,10},{10,1... | collective-permute-start | bytes 1572872 | tf_op jit(solution)/shard_map/ppermute | solution.py:40
  67.3 13.7 %collective-permute-start.23 = (f32[128,8,128]{2,1,0:T(8,128)S(1)}, f32[128,8,128]{2,1,0:T(8,128)S(1)}, u32[]{:S(2)}, u32[]{:S(2)}) collective-permute-start(f32[128,8,128]{2,1,0:T(8,128)S(1)} %get-tuple-element.90), channel_id=1, source_target_pairs={{0,7},{1,0},{2,1},{3,2},{4,3},{5,4},{6,5},{7,6},{8,15},{9,8},{10,9... | collective-permute-start | bytes 1572872 | tf_op jit(solution)/shard_map/ppermute | solution.py:40
  68.2 16.2 %collective-permute-start.13 = (f32[33,8,128]{2,1,0:T(8,128)S(1)}, f32[33,8,128]{2,1,0:T(8,128)S(1)}, u32[]{:S(2)}, u32[]{:S(2)}) collective-permute-start(f32[33,8,128]{2,1,0:T(8,128)S(1)} %get-tuple-element.68), channel_id=1, source_target_pairs={{0,24},{1,25},{2,26},{3,27},{4,28},{5,29},{6,30},{7,31},{8,0},{9,1... | collective-permute-start | bytes 405512 | tf_op jit(solution)/shard_map/ppermute | solution.py:36
  69.0 15.4 %collective-permute-start.9 = (f32[33,8,128]{2,1,0:T(8,128)S(1)}, f32[33,8,128]{2,1,0:T(8,128)S(1)}, u32[]{:S(2)}, u32[]{:S(2)}) collective-permute-start(f32[33,8,128]{2,1,0:T(8,128)S(1)} %get-tuple-element.61), channel_id=1, source_target_pairs={{0,16},{1,17},{2,18},{3,19},{4,20},{5,21},{6,22},{7,23},{8,24},{9,... | collective-permute-start | bytes 405512 | tf_op jit(solution)/shard_map/ppermute | solution.py:36
  70.3 14.2 %collective-permute-start.5 = (f32[33,8,128]{2,1,0:T(8,128)S(1)}, f32[33,8,128]{2,1,0:T(8,128)S(1)}, u32[]{:S(2)}, u32[]{:S(2)}) collective-permute-start(f32[33,8,128]{2,1,0:T(8,128)S(1)} %get-tuple-element.54), channel_id=1, source_target_pairs={{0,8},{1,9},{2,10},{3,11},{4,12},{5,13},{6,14},{7,15},{8,16},{9,17... | collective-permute-start | bytes 405512 | tf_op jit(solution)/shard_map/ppermute | solution.py:36
  73.4 11.1 %copy-start.1 = (s32[128]{0:T(128)S(1)}, s32[128]{0:T(128)}, u32[]{:S(2)}) copy-start(s32[128]{0:T(128)} %param.11) | copy-start | bytes 1540
  81.1 10.5 %collective-permute-start.20 = (f32[128,8,128]{2,1,0:T(8,128)S(1)}, f32[128,8,128]{2,1,0:T(8,128)S(1)}, u32[]{:S(2)}, u32[]{:S(2)}) collective-permute-start(f32[128,8,128]{2,1,0:T(8,128)S(1)} %get-tuple-element.87), channel_id=1, source_target_pairs={{0,1},{1,2},{2,3},{3,4},{4,5},{5,6},{6,7},{7,0},{8,9},{9,10},{10,1... | collective-permute-start | bytes 1572872 | tf_op jit(solution)/shard_map/ppermute | solution.py:40
  83.6 9.2 %collective-permute-start.24 = (f32[128,8,128]{2,1,0:T(8,128)S(1)}, f32[128,8,128]{2,1,0:T(8,128)S(1)}, u32[]{:S(2)}, u32[]{:S(2)}) collective-permute-start(f32[128,8,128]{2,1,0:T(8,128)S(1)} %get-tuple-element.88), channel_id=1, source_target_pairs={{0,7},{1,0},{2,1},{3,2},{4,3},{5,4},{6,5},{7,6},{8,15},{9,8},{10,9... | collective-permute-start | bytes 1572872 | tf_op jit(solution)/shard_map/ppermute | solution.py:40

commit v4 on v3

--- a/solution.py
+++ b/solution.py
@@ -368,8 +368,12 @@
     plus, minus = send_z(dense[4][:half], 1), send_z(dense[4][half:LAND], -1)
     plus, minus = jnp.pad(plus, pad), jnp.pad(minus, (pad[0][::-1], pad[1], pad[2]))
     for k in (3, 2, 1):
-        plus = send_z(dense[k][:LAND] + plus, 1)
-        minus = send_z(dense[k][LAND : 2 * LAND] + minus, -1)
+        own = dense[k]
+        up = own[:LAND] + plus
+        if k in (2,):
+            own, up = lax.optimization_barrier((own, up))
+        down = own[LAND : 2 * LAND] + minus
+        plus, minus = send_z(up, 1), send_z(down, -1)
     total = dense[0][:LAND] + plus + minus
     return total * land_mask.astype(jnp.float32)[:, None, None]
 

time: 93.8 us -> 93.1 us (level)
  waiting for transfers between devices: 23.3 us -> 18.7 us
  starting transfers between devices: 41.3 us -> 44.9 us
    ppermute x8, waiting for transfers between devices: 14.6 us -> 12 us  [send_z(): return lax.ppermute(a, 'tile', shift(0, dz))]
    ppermute x15, starting transfers between devices: 16.1 us -> 18.2 us  [send_x(): return lax.ppermute(a, 'tile', shift(dx, 0))]
    ppermute x15, waiting for transfers between devices: 7.57 us -> 5.59 us  [send_x(): return lax.ppermute(a, 'tile', shift(dx, 0))]
    ppermute x8, starting transfers between devices: 18.9 us -> 20.4 us  [send_z(): return lax.ppermute(a, 'tile', shift(0, dz))]
  transfers between devices with their start and end apart: 25 -> 25, of which waited for: 10 -> 9; matrix products, arithmetic and copies ran while one was open for 1% -> 1% of each run, Pallas kernels for 15% -> 15%
where the time goes in v4:
time: 93.1 us; the launch traced here: 92.9 us
  starting transfers between devices  44.9 us (48%)
  Pallas kernels  25 us (27%)
  waiting for transfers between devices  18.7 us (20%)
  local copies, waits for them, and re-layouts  2.09 us (2%)
  other arithmetic  2.06 us (2%)
    ppermute x8, starting transfers between devices, send_z(): return lax.ppermute(a, 'tile', shift(0, dz))  20.4 us
    ppermute x15, starting transfers between devices, send_x(): return lax.ppermute(a, 'tile', shift(dx, 0))  18.2 us
    ppermute x8, waiting for transfers between devices, send_z(): return lax.ppermute(a, 'tile', shift(0, dz))  12 us
    pallas_call x1, Pallas kernels, remap_far(): pl.pallas_call(far_kernel, out_shape=[jax.ShapeDtypeStruct((ROWS * COLS /...  11.1 us
    pallas_call x1, Pallas kernels, remap_near(): pl.pallas_call(near_kernel, out_shape=shapes, in_specs=[pl.BlockSpec(memo...  7.52 us
    pallas_call x5, Pallas kernels, gather_class(): pl.pallas_call(lambda *refs: gather_kernel(size, *refs), out_shape=jax.Sh...  6.37 us
    ppermute x15, waiting for transfers between devices, send_x(): return lax.ppermute(a, 'tile', shift(dx, 0))  5.59 us
    ppermute x1, starting transfers between devices, body(): lax.ppermute(atmos[:, 0, :], 'tile', [((i + 1) % tiles, i) for i in range...  4.3 us
  transfers between devices with their start and end apart: 25, of which 9 were waited for; matrix products, arithmetic and copies ran while one was open for 1% of the time, Pallas kernels for 15%

profile of v4, /device:TPU:6, one launch (start us, length us, event | category | flops | bytes accessed | tf_op | source)
XLA Modules:
  0.0 92.9 jit_solution(16641409388049958334)
XLA Ops:
  0.0 1.1 %fusion.2 = (f32[8,1,1024]{2,1,0:T(1,128)S(1)}, f32[8,1,1024]{2,1,0:T(1,128)S(1)}) fusion(f32[8,64,1024]{2,1,0:T(8,128)} %param.6), kind=kLoop, calls=%fused_computation.12 | loop fusion | bytes 131072 | tf_op jit(solution)/shard_map/slice | solution.py:352
  1.1 2.0 %collective-permute-start = (f32[8,1024]{1,0:T(8,128)S(1)}, f32[8,1024]{1,0:T(8,128)S(1)}, u32[]{:S(2)}, u32[]{:S(2)}) collective-permute-start(f32[8,1024]{1,0:T(8,128)S(1)} %bitcast.10), channel_id=1, source_target_pairs={{0,1},{1,2},{2,3},{3,4},{4,5},{5,6},{6,7},{7,8},{8,9},{9,10},{10,1... | collective-permute-start | bytes 98312 | tf_op jit(solution)/shard_map/ppermute | solution.py:351
  3.1 4.3 %collective-permute-start.1 = (f32[8,1024]{1,0:T(8,128)S(1)}, f32[8,1024]{1,0:T(8,128)S(1)}, u32[]{:S(2)}, u32[]{:S(2)}) collective-permute-start(f32[8,1024]{1,0:T(8,128)S(1)} %bitcast.11), channel_id=1, source_target_pairs={{1,0},{2,1},{3,2},{4,3},{5,4},{6,5},{7,6},{8,7},{9,8},{10,9},{11,1... | collective-permute-start | bytes 98312 | tf_op jit(solution)/shard_map/ppermute | solution.py:352
  8.1 1.1 %collective-permute-done.north = f32[8,1024]{1,0:T(8,128)S(1)} collective-permute-done((f32[8,1024]{1,0:T(8,128)S(1)}, f32[8,1024]{1,0:T(8,128)S(1)}, u32[]{:S(2)}, u32[]{:S(2)}) %collective-permute-start) | collective-permute-done | bytes 32800 | tf_op jit(solution)/shard_map/ppermute | solution.py:351
  9.2 0.9 %copy-done = f32[64,1024]{1,0:T(8,128)S(1)} copy-done((f32[64,1024]{1,0:T(8,128)S(1)}, f32[64,1024]{1,0:T(8,128)}, u32[]{:S(2)}) %copy-start) | copy-done | bytes 262168
  10.1 11.1 %shard_map.64 = (f32[512,8,128]{2,1,0:T(8,128)S(1)}, s32[6,512]{1,0:T(8,128)S(1)}, f32[33,8,128]{2,1,0:T(8,128)S(1)}, f32[33,8,128]{2,1,0:T(8,128)S(1)}, f32[33,...) custom-call(f32[512,1024]{1,0:T(8,128)} %bitcast.9, ...), custom_call_target="tpu_custom_call" | custom-call | flops 1048576 | bytes 20971520 | tf_op jit(solution)/shard_map/pallas_call | solution.py:258
  21.3 2.5 %collective-permute-start.14 = (f32[33,8,128]{2,1,0:T(8,128)S(1)}, f32[33,8,128]{2,1,0:T(8,128)S(1)}, u32[]{:S(2)}, u32[]{:S(2)}) collective-permute-start(f32[33,8,128]{2,1,0:T(8,128)S(1)} %get-tuple-element.84), channel_id=1, source_target_pairs={{0,8},{1,9},{2,10},{3,11},{4,12},{5,13},{6,14},{7,15},{8,16},{9,17... | collective-permute-start | bytes 405512 | tf_op jit(solution)/shard_map/ppermute | solution.py:36
  24.7 2.5 %collective-permute-start.2 = (f32[65,8,128]{2,1,0:T(8,128)S(1)}, f32[65,8,128]{2,1,0:T(8,128)S(1)}, u32[]{:S(2)}, u32[]{:S(2)}) collective-permute-start(f32[65,8,128]{2,1,0:T(8,128)S(1)} %get-tuple-element.50), channel_id=1, source_target_pairs={{0,8},{1,9},{2,10},{3,11},{4,12},{5,13},{6,14},{7,15},{8,16},{9,17... | collective-permute-start | bytes 798728 | tf_op jit(solution)/shard_map/ppermute | solution.py:36
  27.2 2.1 %collective-permute-start.6 = (f32[65,8,128]{2,1,0:T(8,128)S(1)}, f32[65,8,128]{2,1,0:T(8,128)S(1)}, u32[]{:S(2)}, u32[]{:S(2)}) collective-permute-start(f32[65,8,128]{2,1,0:T(8,128)S(1)} %get-tuple-element.57), channel_id=1, source_target_pairs={{0,16},{1,17},{2,18},{3,19},{4,20},{5,21},{6,22},{7,23},{8,24},{9,... | collective-permute-start | bytes 798728 | tf_op jit(solution)/shard_map/ppermute | solution.py:36
  29.3 7.5 %shard_map.65 = (f32[65,8,128]{2,1,0:T(8,128)S(1)}, f32[65,8,128]{2,1,0:T(8,128)S(1)}, f32[65,8,128]{2,1,0:T(8,128)S(1)}, f32[65,8,128]{2,1,0:T(8,128)S(1)}, f32...) custom-call(s32[6,512]{1,0:T(8,128)S(1)} %get-tuple-element.47.meta,, ...), custom_call_target="tpu_custom_call" | custom-call | flops 8589934592 | bytes 25165824 | tf_op jit(solution)/shard_map/pallas_call | solution.py:291
  37.0 1.0 %shard_map.70 = f32[264,8,128]{2,1,0:T(8,128)S(1)} custom-call(f32[33,8,128]{2,1,0:T(8,128)S(1)} %get-tuple-element.83.refs_0_, f32[33,8,128]{2,1,0:T(8,128)S(1)} %collective-permute-done.14.refs_1_, f32[33,8,128]{2,1,0:T(8,128)S(1)} %collective-permute-done.15.refs_2_, f32[33,8,128]{2,1,0:T(8,128)S(1)} %collective-permute-done.16.refs_3_), custom_call_target="tpu_custom_call" | custom-call | flops 4294967296 | bytes 1048576 | tf_op jit(solution)/shard_map/pallas_call | solution.py:332
  38.1 5.1 %collective-permute-start.21 = (f32[64,8,128]{2,1,0:T(8,128)S(1)}, f32[64,8,128]{2,1,0:T(8,128)S(1)}, u32[]{:S(2)}, u32[]{:S(2)}) collective-permute-start(f32[64,8,128]{2,1,0:T(8,128)S(1)} %get-tuple-element.96), channel_id=1, source_target_pairs={{0,7},{1,0},{2,1},{3,2},{4,3},{5,4},{6,5},{7,6},{8,15},{9,8},{10,9... | collective-permute-start | bytes 786440 | tf_op jit(solution)/shard_map/ppermute | solution.py:40
  43.2 1.4 %collective-permute-done.10.refs_3_ = f32[65,8,128]{2,1,0:T(8,128)S(1)} collective-permute-done((f32[65,8,128]{2,1,0:T(8,128)S(1)}, f32[65,8,128]{2,1,0:T(8,128)S(1)}, u32[]{:S(2)}, u32[]{:S(2)}) %collective-permute-start.10) | collective-permute-done | bytes 266272 | tf_op jit(solution)/shard_map/ppermute | solution.py:36
  44.6 2.0 %collective-permute-start.7 = (f32[65,8,128]{2,1,0:T(8,128)S(1)}, f32[65,8,128]{2,1,0:T(8,128)S(1)}, u32[]{:S(2)}, u32[]{:S(2)}) collective-permute-start(f32[65,8,128]{2,1,0:T(8,128)S(1)} %get-tuple-element.59), channel_id=1, source_target_pairs={{0,16},{1,17},{2,18},{3,19},{4,20},{5,21},{6,22},{7,23},{8,24},{9,... | collective-permute-start | bytes 798728 | tf_op jit(solution)/shard_map/ppermute | solution.py:36
  46.6 1.7 %collective-permute-start.3 = (f32[65,8,128]{2,1,0:T(8,128)S(1)}, f32[65,8,128]{2,1,0:T(8,128)S(1)}, u32[]{:S(2)}, u32[]{:S(2)}) collective-permute-start(f32[65,8,128]{2,1,0:T(8,128)S(1)} %get-tuple-element.52), channel_id=1, source_target_pairs={{0,8},{1,9},{2,10},{3,11},{4,12},{5,13},{6,14},{7,15},{8,16},{9,17... | collective-permute-start | bytes 798728 | tf_op jit(solution)/shard_map/ppermute | solution.py:36
  48.2 1.6 %shard_map.69 = f32[264,8,128]{2,1,0:T(8,128)S(1)} custom-call(f32[65,8,128]{2,1,0:T(8,128)S(1)} %get-tuple-element.79.refs_0_, f32[65,8,128]{2,1,0:T(8,128)S(1)} %collective-permute-done.2.refs_1_, f32[65,8,128]{2,1,0:T(8,128)S(1)} %collective-permute-done.6.refs_2_, f32[65,8,128]{2,1,0:T(8,128)S(1)} %collective-permute-done.10.refs_3_), custom_call_target="tpu_custom_call" | custom-call | flops 4294967296 | bytes 1048576 | tf_op jit(solution)/shard_map/pallas_call | solution.py:332
  50.4 4.0 %collective-permute-start.22 = (f32[128,8,128]{2,1,0:T(8,128)S(1)}, f32[128,8,128]{2,1,0:T(8,128)S(1)}, u32[]{:S(2)}, u32[]{:S(2)}) collective-permute-start(f32[128,8,128]{2,1,0:T(8,128)S(1)} %get-tuple-element.94), channel_id=1, source_target_pairs={{0,7},{1,0},{2,1},{3,2},{4,3},{5,4},{6,5},{7,6},{8,15},{9,8},{10,9... | collective-permute-start | bytes 1572872 | tf_op jit(solution)/shard_map/ppermute | solution.py:40
  54.6 3.8 %collective-permute-done.7.refs_2_ = f32[65,8,128]{2,1,0:T(8,128)S(1)} collective-permute-done((f32[65,8,128]{2,1,0:T(8,128)S(1)}, f32[65,8,128]{2,1,0:T(8,128)S(1)}, u32[]{:S(2)}, u32[]{:S(2)}) %collective-permute-start.7) | collective-permute-done | bytes 266272 | tf_op jit(solution)/shard_map/ppermute | solution.py:36
  58.4 0.9 collective-permute-start.8
  59.5 2.2 %collective-permute-start.4 = (f32[65,8,128]{2,1,0:T(8,128)S(1)}, f32[65,8,128]{2,1,0:T(8,128)S(1)}, u32[]{:S(2)}, u32[]{:S(2)}) collective-permute-start(f32[65,8,128]{2,1,0:T(8,128)S(1)} %get-tuple-element.54), channel_id=1, source_target_pairs={{0,8},{1,9},{2,10},{3,11},{4,12},{5,13},{6,14},{7,15},{8,16},{9,17... | collective-permute-start | bytes 798728 | tf_op jit(solution)/shard_map/ppermute | solution.py:36
  61.7 1.3 %shard_map.68 = f32[264,8,128]{2,1,0:T(8,128)S(1)} custom-call(f32[65,8,128]{2,1,0:T(8,128)S(1)} %get-tuple-element.75.refs_0_, f32[65,8,128]{2,1,0:T(8,128)S(1)} %collective-permute-done.3.refs_1_, f32[65,8,128]{2,1,0:T(8,128)S(1)} %collective-permute-done.7.refs_2_, f32[65,8,128]{2,1,0:T(8,128)S(1)} %collective-permute-done.11.refs_3_), custom_call_target="tpu_custom_call" | custom-call | flops 4294967296 | bytes 1048576 | tf_op jit(solution)/shard_map/pallas_call | solution.py:332
  63.1 1.1 %collective-permute-start.19 = (f32[128,8,128]{2,1,0:T(8,128)S(1)}, f32[128,8,128]{2,1,0:T(8,128)S(1)}, u32[]{:S(2)}, u32[]{:S(2)}) collective-permute-start(f32[128,8,128]{2,1,0:T(8,128)S(1)} %slice_add_fusion.3), channel_id=1, source_target_pairs={{0,1},{1,2},{2,3},{3,4},{4,5},{5,6},{6,7},{7,0},{8,9},{9,10},{10,1... | collective-permute-start | bytes 1572872 | tf_op jit(solution)/shard_map/ppermute | solution.py:40
  64.3 5.8 %collective-permute-start.23 = (f32[128,8,128]{2,1,0:T(8,128)S(1)}, f32[128,8,128]{2,1,0:T(8,128)S(1)}, u32[]{:S(2)}, u32[]{:S(2)}) collective-permute-start(f32[128,8,128]{2,1,0:T(8,128)S(1)} %slice_add_fusion.6), channel_id=1, source_target_pairs={{0,7},{1,0},{2,1},{3,2},{4,3},{5,4},{6,5},{7,6},{8,15},{9,8},{10,9... | collective-permute-start | bytes 1572872 | tf_op jit(solution)/shard_map/ppermute | solution.py:40
  70.1 1.5 %collective-permute-start.9 = (f32[33,8,128]{2,1,0:T(8,128)S(1)}, f32[33,8,128]{2,1,0:T(8,128)S(1)}, u32[]{:S(2)}, u32[]{:S(2)}) collective-permute-start(f32[33,8,128]{2,1,0:T(8,128)S(1)} %get-tuple-element.63), channel_id=1, source_target_pairs={{0,16},{1,17},{2,18},{3,19},{4,20},{5,21},{6,22},{7,23},{8,24},{9,... | collective-permute-start | bytes 405512 | tf_op jit(solution)/shard_map/ppermute | solution.py:36
  71.6 1.9 %collective-permute-start.5 = (f32[33,8,128]{2,1,0:T(8,128)S(1)}, f32[33,8,128]{2,1,0:T(8,128)S(1)}, u32[]{:S(2)}, u32[]{:S(2)}) collective-permute-start(f32[33,8,128]{2,1,0:T(8,128)S(1)} %get-tuple-element.56), channel_id=1, source_target_pairs={{0,8},{1,9},{2,10},{3,11},{4,12},{5,13},{6,14},{7,15},{8,16},{9,17... | collective-permute-start | bytes 405512 | tf_op jit(solution)/shard_map/ppermute | solution.py:36
  73.4 1.3 %shard_map.67 = f32[264,8,128]{2,1,0:T(8,128)S(1)} custom-call(f32[65,8,128]{2,1,0:T(8,128)S(1)} %get-tuple-element.71.refs_0_, f32[65,8,128]{2,1,0:T(8,128)S(1)} %collective-permute-done.4.refs_1_, f32[65,8,128]{2,1,0:T(8,128)S(1)} %collective-permute-done.8.refs_2_, f32[65,8,128]{2,1,0:T(8,128)S(1)} %collective-permute-done.12.refs_3_), custom_call_target="tpu_custom_call" | custom-call | flops 4294967296 | bytes 1048576 | tf_op jit(solution)/shard_map/pallas_call | solution.py:332
  74.8 5.8 %collective-permute-done.19 = f32[128,8,128]{2,1,0:T(8,128)S(1)} collective-permute-done((f32[128,8,128]{2,1,0:T(8,128)S(1)}, f32[128,8,128]{2,1,0:T(8,128)S(1)}, u32[]{:S(2)}, u32[]{:S(2)}) %collective-permute-start.19) | collective-permute-done | bytes 524320 | tf_op jit(solution)/shard_map/ppermute | solution.py:40
  80.8 1.1 %collective-permute-start.20 = (f32[128,8,128]{2,1,0:T(8,128)S(1)}, f32[128,8,128]{2,1,0:T(8,128)S(1)}, u32[]{:S(2)}, u32[]{:S(2)}) collective-permute-start(f32[128,8,128]{2,1,0:T(8,128)S(1)} %get-tuple-element.91), channel_id=1, source_target_pairs={{0,1},{1,2},{2,3},{3,4},{4,5},{5,6},{6,7},{7,0},{8,9},{9,10},{10,1... | collective-permute-start | bytes 1572872 | tf_op jit(solution)/shard_map/ppermute | solution.py:40
  81.9 2.8 %collective-permute-start.24 = (f32[128,8,128]{2,1,0:T(8,128)S(1)}, f32[128,8,128]{2,1,0:T(8,128)S(1)}, u32[]{:S(2)}, u32[]{:S(2)}) collective-permute-start(f32[128,8,128]{2,1,0:T(8,128)S(1)} %get-tuple-element.92), channel_id=1, source_target_pairs={{0,7},{1,0},{2,1},{3,2},{4,3},{5,4},{6,5},{7,6},{8,15},{9,8},{10,9... | collective-permute-start | bytes 1572872 | tf_op jit(solution)/shard_map/ppermute | solution.py:40
  84.7 1.1 %shard_map.66 = f32[264,8,128]{2,1,0:T(8,128)S(1)} custom-call(f32[33,8,128]{2,1,0:T(8,128)S(1)} %get-tuple-element.49.refs_0_, f32[33,8,128]{2,1,0:T(8,128)S(1)} %collective-permute-done.5.refs_1_, f32[33,8,128]{2,1,0:T(8,128)S(1)} %collective-permute-done.9.refs_2_, f32[33,8,128]{2,1,0:T(8,128)S(1)} %collective-permute-done.13.refs_3_), custom_call_target="tpu_custom_call" | custom-call | flops 4294967296 | bytes 1048576 | tf_op jit(solution)/shard_map/pallas_call | solution.py:332
  85.8 5.9 %collective-permute-done.20 = f32[128,8,128]{2,1,0:T(8,128)S(1)} collective-permute-done((f32[128,8,128]{2,1,0:T(8,128)S(1)}, f32[128,8,128]{2,1,0:T(8,128)S(1)}, u32[]{:S(2)}, u32[]{:S(2)}) %collective-permute-start.20) | collective-permute-done | bytes 524320 | tf_op jit(solution)/shard_map/ppermute | solution.py:40
  91.9 1.0 %fusion.1 = f32[128,8,128]{2,1,0:T(8,128)} fusion(f32[128,8,128]{2,1,0:T(8,128)S(1)} %collective-permute-done.24, f32[128,8,128]{2,1,0:T(8,128)S(1)} %collective-permute-done.20, f32[264,8,128]{2,1,0:T(8,128)S(1)} %shard_map.66, f32[128]{0:T(128)S(1)} %convert_element_type.7), kind=kLoop, calls=%fused_computation.7 | loop fusion | flops 393216 | bytes 2097664 | tf_op jit(solution)/shard_map/mul | solution.py:378
  (40 shorter events, 3.4 us)
Async XLA Ops:
  1.1 8.1 %collective-permute-start = (f32[8,1024]{1,0:T(8,128)S(1)}, f32[8,1024]{1,0:T(8,128)S(1)}, u32[]{:S(2)}, u32[]{:S(2)}) collective-permute-start(f32[8,1024]{1,0:T(8,128)S(1)} %bitcast.10), channel_id=1, source_target_pairs={{0,1},{1,2},{2,3},{3,4},{4,5},{5,6},{6,7},{7,8},{8,9},{9,10},{10,1... | collective-permute-start | bytes 98312 | tf_op jit(solution)/shard_map/ppermute | solution.py:351
  3.1 6.1 %collective-permute-start.1 = (f32[8,1024]{1,0:T(8,128)S(1)}, f32[8,1024]{1,0:T(8,128)S(1)}, u32[]{:S(2)}, u32[]{:S(2)}) collective-permute-start(f32[8,1024]{1,0:T(8,128)S(1)} %bitcast.11), channel_id=1, source_target_pairs={{1,0},{2,1},{3,2},{4,3},{5,4},{6,5},{7,6},{8,7},{9,8},{10,9},{11,1... | collective-permute-start | bytes 98312 | tf_op jit(solution)/shard_map/ppermute | solution.py:352
  9.2 1.0 %copy-start = (f32[64,1024]{1,0:T(8,128)S(1)}, f32[64,1024]{1,0:T(8,128)}, u32[]{:S(2)}) copy-start(f32[64,1024]{1,0:T(8,128)} %kappa.1) | copy-start | bytes 786436
  21.3 15.6 %collective-permute-start.14 = (f32[33,8,128]{2,1,0:T(8,128)S(1)}, f32[33,8,128]{2,1,0:T(8,128)S(1)}, u32[]{:S(2)}, u32[]{:S(2)}) collective-permute-start(f32[33,8,128]{2,1,0:T(8,128)S(1)} %get-tuple-element.84), channel_id=1, source_target_pairs={{0,8},{1,9},{2,10},{3,11},{4,12},{5,13},{6,14},{7,15},{8,16},{9,17... | collective-permute-start | bytes 405512 | tf_op jit(solution)/shard_map/ppermute | solution.py:36
  23.8 13.2 %collective-permute-start.15 = (f32[33,8,128]{2,1,0:T(8,128)S(1)}, f32[33,8,128]{2,1,0:T(8,128)S(1)}, u32[]{:S(2)}, u32[]{:S(2)}) collective-permute-start(f32[33,8,128]{2,1,0:T(8,128)S(1)} %get-tuple-element.85), channel_id=1, source_target_pairs={{0,16},{1,17},{2,18},{3,19},{4,20},{5,21},{6,22},{7,23},{8,24},{9,... | collective-permute-start | bytes 405512 | tf_op jit(solution)/shard_map/ppermute | solution.py:36
  24.0 13.0 %collective-permute-start.16 = (f32[33,8,128]{2,1,0:T(8,128)S(1)}, f32[33,8,128]{2,1,0:T(8,128)S(1)}, u32[]{:S(2)}, u32[]{:S(2)}) collective-permute-start(f32[33,8,128]{2,1,0:T(8,128)S(1)} %get-tuple-element.86), channel_id=1, source_target_pairs={{0,24},{1,25},{2,26},{3,27},{4,28},{5,29},{6,30},{7,31},{8,0},{9,1... | collective-permute-start | bytes 405512 | tf_op jit(solution)/shard_map/ppermute | solution.py:36
  24.7 18.5 %collective-permute-start.2 = (f32[65,8,128]{2,1,0:T(8,128)S(1)}, f32[65,8,128]{2,1,0:T(8,128)S(1)}, u32[]{:S(2)}, u32[]{:S(2)}) collective-permute-start(f32[65,8,128]{2,1,0:T(8,128)S(1)} %get-tuple-element.50), channel_id=1, source_target_pairs={{0,8},{1,9},{2,10},{3,11},{4,12},{5,13},{6,14},{7,15},{8,16},{9,17... | collective-permute-start | bytes 798728 | tf_op jit(solution)/shard_map/ppermute | solution.py:36
  27.2 16.0 %collective-permute-start.6 = (f32[65,8,128]{2,1,0:T(8,128)S(1)}, f32[65,8,128]{2,1,0:T(8,128)S(1)}, u32[]{:S(2)}, u32[]{:S(2)}) collective-permute-start(f32[65,8,128]{2,1,0:T(8,128)S(1)} %get-tuple-element.57), channel_id=1, source_target_pairs={{0,16},{1,17},{2,18},{3,19},{4,20},{5,21},{6,22},{7,23},{8,24},{9,... | collective-permute-start | bytes 798728 | tf_op jit(solution)/shard_map/ppermute | solution.py:36
  36.9 7.7 %collective-permute-start.10 = (f32[65,8,128]{2,1,0:T(8,128)S(1)}, f32[65,8,128]{2,1,0:T(8,128)S(1)}, u32[]{:S(2)}, u32[]{:S(2)}) collective-permute-start(f32[65,8,128]{2,1,0:T(8,128)S(1)} %get-tuple-element.64), channel_id=1, source_target_pairs={{0,24},{1,25},{2,26},{3,27},{4,28},{5,29},{6,30},{7,31},{8,0},{9,1... | collective-permute-start | bytes 798728 | tf_op jit(solution)/shard_map/ppermute | solution.py:36
  38.0 11.8 %collective-permute-start.17 = (f32[64,8,128]{2,1,0:T(8,128)S(1)}, f32[64,8,128]{2,1,0:T(8,128)S(1)}, u32[]{:S(2)}, u32[]{:S(2)}) collective-permute-start(f32[64,8,128]{2,1,0:T(8,128)S(1)} %get-tuple-element.95), channel_id=1, source_target_pairs={{0,1},{1,2},{2,3},{3,4},{4,5},{5,6},{6,7},{7,0},{8,9},{9,10},{10,1... | collective-permute-start | bytes 786440 | tf_op jit(solution)/shard_map/ppermute | solution.py:40
  38.1 11.7 %collective-permute-start.21 = (f32[64,8,128]{2,1,0:T(8,128)S(1)}, f32[64,8,128]{2,1,0:T(8,128)S(1)}, u32[]{:S(2)}, u32[]{:S(2)}) collective-permute-start(f32[64,8,128]{2,1,0:T(8,128)S(1)} %get-tuple-element.96), channel_id=1, source_target_pairs={{0,7},{1,0},{2,1},{3,2},{4,3},{5,4},{6,5},{7,6},{8,15},{9,8},{10,9... | collective-permute-start | bytes 786440 | tf_op jit(solution)/shard_map/ppermute | solution.py:40
  44.6 10.1 %collective-permute-start.11 = (f32[65,8,128]{2,1,0:T(8,128)S(1)}, f32[65,8,128]{2,1,0:T(8,128)S(1)}, u32[]{:S(2)}, u32[]{:S(2)}) collective-permute-start(f32[65,8,128]{2,1,0:T(8,128)S(1)} %get-tuple-element.66), channel_id=1, source_target_pairs={{0,24},{1,25},{2,26},{3,27},{4,28},{5,29},{6,30},{7,31},{8,0},{9,1... | collective-permute-start | bytes 798728 | tf_op jit(solution)/shard_map/ppermute | solution.py:36
  44.6 13.8 %collective-permute-start.7 = (f32[65,8,128]{2,1,0:T(8,128)S(1)}, f32[65,8,128]{2,1,0:T(8,128)S(1)}, u32[]{:S(2)}, u32[]{:S(2)}) collective-permute-start(f32[65,8,128]{2,1,0:T(8,128)S(1)} %get-tuple-element.59), channel_id=1, source_target_pairs={{0,16},{1,17},{2,18},{3,19},{4,20},{5,21},{6,22},{7,23},{8,24},{9,... | collective-permute-start | bytes 798728 | tf_op jit(solution)/shard_map/ppermute | solution.py:36
  46.6 12.9 %collective-permute-start.3 = (f32[65,8,128]{2,1,0:T(8,128)S(1)}, f32[65,8,128]{2,1,0:T(8,128)S(1)}, u32[]{:S(2)}, u32[]{:S(2)}) collective-permute-start(f32[65,8,128]{2,1,0:T(8,128)S(1)} %get-tuple-element.52), channel_id=1, source_target_pairs={{0,8},{1,9},{2,10},{3,11},{4,12},{5,13},{6,14},{7,15},{8,16},{9,17... | collective-permute-start | bytes 798728 | tf_op jit(solution)/shard_map/ppermute | solution.py:36
  49.9 13.1 %collective-permute-start.18 = (f32[128,8,128]{2,1,0:T(8,128)S(1)}, f32[128,8,128]{2,1,0:T(8,128)S(1)}, u32[]{:S(2)}, u32[]{:S(2)}) collective-permute-start(f32[128,8,128]{2,1,0:T(8,128)S(1)} %get-tuple-element.93), channel_id=1, source_target_pairs={{0,1},{1,2},{2,3},{3,4},{4,5},{5,6},{6,7},{7,0},{8,9},{9,10},{10,1... | collective-permute-start | bytes 1572872 | tf_op jit(solution)/shard_map/ppermute | solution.py:40
  50.4 13.8 %collective-permute-start.22 = (f32[128,8,128]{2,1,0:T(8,128)S(1)}, f32[128,8,128]{2,1,0:T(8,128)S(1)}, u32[]{:S(2)}, u32[]{:S(2)}) collective-permute-start(f32[128,8,128]{2,1,0:T(8,128)S(1)} %get-tuple-element.94), channel_id=1, source_target_pairs={{0,7},{1,0},{2,1},{3,2},{4,3},{5,4},{6,5},{7,6},{8,15},{9,8},{10,9... | collective-permute-start | bytes 1572872 | tf_op jit(solution)/shard_map/ppermute | solution.py:40
  54.6 15.5 %collective-permute-start.12 = (f32[65,8,128]{2,1,0:T(8,128)S(1)}, f32[65,8,128]{2,1,0:T(8,128)S(1)}, u32[]{:S(2)}, u32[]{:S(2)}) collective-permute-start(f32[65,8,128]{2,1,0:T(8,128)S(1)} %get-tuple-element.68), channel_id=1, source_target_pairs={{0,24},{1,25},{2,26},{3,27},{4,28},{5,29},{6,30},{7,31},{8,0},{9,1... | collective-permute-start | bytes 798728 | tf_op jit(solution)/shard_map/ppermute | solution.py:36
  58.4 11.7 %collective-permute-start.8 = (f32[65,8,128]{2,1,0:T(8,128)S(1)}, f32[65,8,128]{2,1,0:T(8,128)S(1)}, u32[]{:S(2)}, u32[]{:S(2)}) collective-permute-start(f32[65,8,128]{2,1,0:T(8,128)S(1)} %get-tuple-element.61), channel_id=1, source_target_pairs={{0,16},{1,17},{2,18},{3,19},{4,20},{5,21},{6,22},{7,23},{8,24},{9,... | collective-permute-start | bytes 798728 | tf_op jit(solution)/shard_map/ppermute | solution.py:36
  59.5 12.1 %collective-permute-start.4 = (f32[65,8,128]{2,1,0:T(8,128)S(1)}, f32[65,8,128]{2,1,0:T(8,128)S(1)}, u32[]{:S(2)}, u32[]{:S(2)}) collective-permute-start(f32[65,8,128]{2,1,0:T(8,128)S(1)} %get-tuple-element.54), channel_id=1, source_target_pairs={{0,8},{1,9},{2,10},{3,11},{4,12},{5,13},{6,14},{7,15},{8,16},{9,17... | collective-permute-start | bytes 798728 | tf_op jit(solution)/shard_map/ppermute | solution.py:36
  63.1 17.5 %collective-permute-start.19 = (f32[128,8,128]{2,1,0:T(8,128)S(1)}, f32[128,8,128]{2,1,0:T(8,128)S(1)}, u32[]{:S(2)}, u32[]{:S(2)}) collective-permute-start(f32[128,8,128]{2,1,0:T(8,128)S(1)} %slice_add_fusion.3), channel_id=1, source_target_pairs={{0,1},{1,2},{2,3},{3,4},{4,5},{5,6},{6,7},{7,0},{8,9},{9,10},{10,1... | collective-permute-start | bytes 1572872 | tf_op jit(solution)/shard_map/ppermute | solution.py:40
  64.3 16.4 %collective-permute-start.23 = (f32[128,8,128]{2,1,0:T(8,128)S(1)}, f32[128,8,128]{2,1,0:T(8,128)S(1)}, u32[]{:S(2)}, u32[]{:S(2)}) collective-permute-start(f32[128,8,128]{2,1,0:T(8,128)S(1)} %slice_add_fusion.6), channel_id=1, source_target_pairs={{0,7},{1,0},{2,1},{3,2},{4,3},{5,4},{6,5},{7,6},{8,15},{9,8},{10,9... | collective-permute-start | bytes 1572872 | tf_op jit(solution)/shard_map/ppermute | solution.py:40
  70.1 14.6 %collective-permute-start.13 = (f32[33,8,128]{2,1,0:T(8,128)S(1)}, f32[33,8,128]{2,1,0:T(8,128)S(1)}, u32[]{:S(2)}, u32[]{:S(2)}) collective-permute-start(f32[33,8,128]{2,1,0:T(8,128)S(1)} %get-tuple-element.70), channel_id=1, source_target_pairs={{0,24},{1,25},{2,26},{3,27},{4,28},{5,29},{6,30},{7,31},{8,0},{9,1... | collective-permute-start | bytes 405512 | tf_op jit(solution)/shard_map/ppermute | solution.py:36
  70.1 14.6 %collective-permute-start.9 = (f32[33,8,128]{2,1,0:T(8,128)S(1)}, f32[33,8,128]{2,1,0:T(8,128)S(1)}, u32[]{:S(2)}, u32[]{:S(2)}) collective-permute-start(f32[33,8,128]{2,1,0:T(8,128)S(1)} %get-tuple-element.63), channel_id=1, source_target_pairs={{0,16},{1,17},{2,18},{3,19},{4,20},{5,21},{6,22},{7,23},{8,24},{9,... | collective-permute-start | bytes 405512 | tf_op jit(solution)/shard_map/ppermute | solution.py:36
  71.6 13.1 %collective-permute-start.5 = (f32[33,8,128]{2,1,0:T(8,128)S(1)}, f32[33,8,128]{2,1,0:T(8,128)S(1)}, u32[]{:S(2)}, u32[]{:S(2)}) collective-permute-start(f32[33,8,128]{2,1,0:T(8,128)S(1)} %get-tuple-element.56), channel_id=1, source_target_pairs={{0,8},{1,9},{2,10},{3,11},{4,12},{5,13},{6,14},{7,15},{8,16},{9,17... | collective-permute-start | bytes 405512 | tf_op jit(solution)/shard_map/ppermute | solution.py:36
  74.8 9.9 %copy-start.1 = (s32[128]{0:T(128)S(1)}, s32[128]{0:T(128)}, u32[]{:S(2)}) copy-start(s32[128]{0:T(128)} %param.11) | copy-start | bytes 1540
  80.8 10.9 %collective-permute-start.20 = (f32[128,8,128]{2,1,0:T(8,128)S(1)}, f32[128,8,128]{2,1,0:T(8,128)S(1)}, u32[]{:S(2)}, u32[]{:S(2)}) collective-permute-start(f32[128,8,128]{2,1,0:T(8,128)S(1)} %get-tuple-element.91), channel_id=1, source_target_pairs={{0,1},{1,2},{2,3},{3,4},{4,5},{5,6},{6,7},{7,0},{8,9},{9,10},{10,1... | collective-permute-start | bytes 1572872 | tf_op jit(solution)/shard_map/ppermute | solution.py:40
  81.9 10.0 %collective-permute-start.24 = (f32[128,8,128]{2,1,0:T(8,128)S(1)}, f32[128,8,128]{2,1,0:T(8,128)S(1)}, u32[]{:S(2)}, u32[]{:S(2)}) collective-permute-start(f32[128,8,128]{2,1,0:T(8,128)S(1)} %get-tuple-element.92), channel_id=1, source_target_pairs={{0,7},{1,0},{2,1},{3,2},{4,3},{5,4},{6,5},{7,6},{8,15},{9,8},{10,9... | collective-permute-start | bytes 1572872 | tf_op jit(solution)/shard_map/ppermute | solution.py:40
